TPU v7x, 32 devices: a whole 2x2x4 slice. The times are simulated.
32 devices in a mesh: pb: 8 (over z, x), ka: 4 (over y, core).
Axes of the slice: x: 2, y: 2, z: 4, core: 2. Of those that a mesh axis runs over, the one named last changes fastest.
Arguments:
- tokens: bfloat16 [4096, 768], P(('pb', 'ka')), may hold values from -6 to 6
- cotangent: bfloat16 [4096, 768], P(('pb', 'ka')), may hold values from -6 to 6
- lengths: int32 [8, 3], P('pb'), may hold values from 1 to 384, 512 in all within a row
- keep_mask: int32 [4096], P(('pb', 'ka')), may hold values 0 or 1
- w_qkv: bfloat16 [768, 2, 2304], P('pb'), may hold values from -0.21875 to 0.21875
- w_out: bfloat16 [768, 2, 768], P('pb'), may hold values from -0.875 to 0.875
- w_fc: bfloat16 [768, 2, 3072], P('pb'), may hold values from -0.21875 to 0.21875
- w_proj: bfloat16 [3072, 2, 768], P('pb'), may hold values from -0.21875 to 0.21875
- norm_gain: bfloat16 [768, 4], P('pb'), may hold values from 0.5 to 1.5
- norm_bias: bfloat16 [768, 4], P('pb'), may hold values from -1.75 to 1.75
Outputs:
- output: bfloat16 [4096, 768], P(('pb', 'ka'))
- grad_tokens: float32 [4096, 768], P(('pb', 'ka'))
- grad_w_qkv: float32 [768, 2, 2304], P('pb')
- grad_w_out: float32 [768, 2, 768], P('pb')
- grad_w_fc: float32 [768, 2, 3072], P('pb')
- grad_w_proj: float32 [3072, 2, 768], P('pb')
- grad_norm_gain: float32 [768, 4], P('pb')
- grad_norm_bias: float32 [768, 4], P('pb')
Inputs may be any that keep to these rules, and one draw needn't show every extreme that they name: Row g of lengths lists the 3 sequences of group g in order; they sum to 512, and the longest of each row has exactly 384 tokens. `keep_mask`: A padding token is read by no other token.
All inputs are finite; a program needn't handle non-finite values. No bound on the sum of `keep_mask` on one device may be relied on, other than what follows from the above.
Results may differ from a plain program's by a relative error of at most 0.034.
Values may be sent and summed in bfloat16 or wider, within the bound.
No kernel may reach another device: no remote copies, remote signals or barrier semaphores. Data moves between devices by JAX's collectives and lax.ppermute only.
A program may use at most 320 MiB of HBM per device.

v0:
```python
import jax
import jax.numpy as jnp
from jax import lax
from jax.sharding import PartitionSpec as P

H = 12


EPSILON = 1e-05
FLOOR_VALUE = -1e30


def merged(x, axis, join):
    gathered = jax.tree.map(
        lambda a, kind: lax.all_gather(a.astype(kind), axis), x, (jnp.bfloat16, jnp.bfloat16)
    )

    def take(source):
        return jax.tree.map(
            lambda a, own: lax.dynamic_index_in_dim(a, source, 0, False).astype(own.dtype),
            gathered,
            x,
        )

    return lax.fori_loop(
        1, lax.axis_size(axis), lambda source, state: join(state, take(source)), take(0)
    )


def norm_forward(values, gain_row, offset):
    average = jnp.mean(values, axis=-1, keepdims=True)
    centered = values - average
    spread = jnp.mean(centered * centered, axis=-1, keepdims=True)
    inverse = lax.rsqrt(spread + EPSILON)
    normal = centered * inverse
    return (normal * gain_row + offset, normal, inverse)


def norm_backward(grad_out, normal, inverse, gain_row):
    grad_normal = grad_out * gain_row
    mean_grad = jnp.mean(grad_normal, axis=-1, keepdims=True)
    mean_cross = jnp.mean(grad_normal * normal, axis=-1, keepdims=True)
    return inverse * (grad_normal - mean_grad - normal * mean_cross)


def outer_sum(left, right):
    return lax.dot_general(
        left, right, (((0,), (0,)), ((), ())), preferred_element_type=jnp.float32
    )


def gelu_tanh(hidden_in):
    return jax.nn.gelu(hidden_in, approximate=True)


def block_mask(row_start, block_rows, context):
    segment_all, segment_keys, key_place, key_kept = context
    query_place = row_start + jnp.arange(block_rows, dtype=jnp.int32)
    same_sequence = segment_all[:, None] == segment_keys[None, :]
    causal = key_place[None, :] <= query_place[:, None]
    itself = key_place[None, :] == query_place[:, None]
    return same_sequence & causal & (key_kept[None, :] | itself)


def block_scores(query_block, key_rows, allowed, signed, score_scale):
    scores = (
        jnp.einsum("qhd,khd->hqk", query_block, key_rows, preferred_element_type=jnp.float32)
        * score_scale
    )
    magnitude = jnp.abs(scores) if signed else scores
    masked = jnp.where(allowed[None], magnitude, FLOOR_VALUE)
    return (scores, masked)


def join_stats(first_pair, second_pair):
    row_peak = jnp.maximum(first_pair[0], second_pair[0])
    row_total = first_pair[1] * jnp.exp(first_pair[0] - row_peak) + second_pair[1] * jnp.exp(
        second_pair[0] - row_peak
    )
    return (row_peak, row_total)


def attend_forward(query_all, key_rows, values, context, signed):
    group_rows = query_all.shape[0]
    block_rows = min(512, group_rows)
    score_scale = query_all.shape[2] ** (-0.5)

    def one_block(block_index):
        row_start = block_index * block_rows
        allowed = block_mask(row_start, block_rows, context)
        allowed_float = allowed.astype(jnp.float32)[None]
        scores, masked = block_scores(query_all, key_rows, allowed, signed, score_scale)
        local_peak = jnp.max(masked, axis=-1)
        local_total = jnp.sum(jnp.exp(masked - local_peak[..., None]) * allowed_float, axis=-1)
        row_peak, row_total = merged((local_peak, local_total), "ka", join_stats)
        raised = jnp.exp(masked - row_peak[..., None])
        if signed:
            numerator = jnp.sign(scores) * (raised - jnp.exp(-row_peak)[..., None] * allowed_float)
        else:
            numerator = raised
        weights_low = (numerator / row_total[..., None]).astype(jnp.bfloat16)
        partial_value = jnp.einsum(
            "hqk,khd->qhd", weights_low, values, preferred_element_type=jnp.float32
        )
        return (partial_value.reshape(block_rows, -1), row_peak, row_total)

    partials, peaks, totals = lax.map(
        one_block, jnp.arange(group_rows // block_rows, dtype=jnp.int32)
    )
    return (partials.reshape(group_rows, -1), peaks, totals)


def attend_backward(query_all, grad_all, key_rows, values, peaks, totals, context, signed):
    group_rows = query_all.shape[0]
    block_rows = min(512, group_rows)
    score_scale = query_all.shape[2] ** (-0.5)

    def one_block(running, block_index):
        grad_keys, grad_values = running
        row_start = block_index * block_rows
        allowed = block_mask(row_start, block_rows, context)
        allowed_float = allowed.astype(jnp.float32)[None]
        scores, masked = block_scores(query_all, key_rows, allowed, signed, score_scale)
        row_peak = peaks[block_index]
        row_total = totals[block_index]
        raised = jnp.exp(masked - row_peak[..., None])
        absolute = raised / row_total[..., None]
        if signed:
            signs = jnp.sign(scores)
            weights = (
                signs
                * (raised - jnp.exp(-row_peak)[..., None] * allowed_float)
                / row_total[..., None]
            )
        else:
            signs = 1.0
            weights = absolute
        grad_weights = jnp.einsum(
            "qhd,khd->hqk", grad_all, values, preferred_element_type=jnp.float32
        )
        row_delta = lax.psum(jnp.sum(grad_weights * weights, axis=-1), "ka")
        grad_scores = (absolute * (grad_weights - signs * row_delta[..., None])).astype(
            jnp.bfloat16
        )
        grad_query = (
            jnp.einsum("hqk,khd->qhd", grad_scores, key_rows, preferred_element_type=jnp.float32)
            * score_scale
        )
        grad_keys = (
            grad_keys
            + jnp.einsum("hqk,qhd->khd", grad_scores, query_all, preferred_element_type=jnp.float32)
            * score_scale
        )
        grad_values = grad_values + jnp.einsum(
            "hqk,qhd->khd",
            weights.astype(jnp.bfloat16),
            grad_all,
            preferred_element_type=jnp.float32,
        )
        return ((grad_keys, grad_values), grad_query.reshape(block_rows, -1))

    zero_rows = jnp.zeros(key_rows.shape, jnp.float32)
    (grad_keys, grad_values), grad_queries = lax.scan(
        one_block, (zero_rows, zero_rows), jnp.arange(group_rows // block_rows, dtype=jnp.int32)
    )
    return (grad_keys, grad_values, grad_queries.reshape(group_rows, -1))


def project_inputs(stream, gathered, layer_index, head_count):
    w_qkv = gathered[0]
    gains = gathered[4].astype(jnp.float32)
    offsets = gathered[5].astype(jnp.float32)
    token_rows, model_width = stream.shape
    normed, normal, inverse = norm_forward(
        stream, gains[:, 2 * layer_index], offsets[:, 2 * layer_index]
    )
    normed = normed.astype(jnp.bfloat16)
    projected = jnp.dot(normed, w_qkv[:, layer_index], preferred_element_type=jnp.float32).astype(
        jnp.bfloat16
    )
    query_flat = projected[:, :model_width]
    key_rows = projected[:, model_width : 2 * model_width].reshape(token_rows, head_count, -1)
    values = projected[:, 2 * model_width :].reshape(token_rows, head_count, -1)
    return (normed, normal, inverse, query_flat, key_rows, values)


def feed_inputs(middle, gathered, layer_index):
    w_fc = gathered[2]
    gains = gathered[4].astype(jnp.float32)
    offsets = gathered[5].astype(jnp.float32)
    normed_two, normal_two, inverse_two = norm_forward(
        middle, gains[:, 2 * layer_index + 1], offsets[:, 2 * layer_index + 1]
    )
    normed_two = normed_two.astype(jnp.bfloat16)
    hidden = jnp.dot(normed_two, w_fc[:, layer_index], preferred_element_type=jnp.float32)
    return (normed_two, normal_two, inverse_two, hidden)


def layer_forward(stream, gathered, layer_index, context, head_count):
    w_out = gathered[1]
    w_proj = gathered[3]
    normed, normal, inverse, query_flat, key_rows, values = project_inputs(
        stream, gathered, layer_index, head_count
    )
    query_all = lax.all_gather(query_flat, "ka", axis=0, tiled=True)
    query_all = query_all.reshape(query_all.shape[0], head_count, -1)
    partials, peaks, totals = attend_forward(query_all, key_rows, values, context, layer_index == 0)
    attended_full = lax.psum_scatter(
        partials.astype(jnp.bfloat16), "ka", scatter_dimension=0, tiled=True
    ).astype(jnp.float32)
    attended = attended_full.astype(jnp.bfloat16)
    middle = stream + jnp.dot(attended, w_out[:, layer_index], preferred_element_type=jnp.float32)
    normed_two, normal_two, inverse_two, hidden = feed_inputs(middle, gathered, layer_index)
    active = gelu_tanh(hidden).astype(jnp.bfloat16)
    result = middle + jnp.dot(active, w_proj[:, layer_index], preferred_element_type=jnp.float32)
    return (result, (attended, peaks, totals, middle, attended_full))


def layer_backward(grad_stream, stream, kept_state, gathered, layer_index, context, head_count):
    w_qkv, w_out, w_fc, w_proj = (gathered[0], gathered[1], gathered[2], gathered[3])
    gains = gathered[4].astype(jnp.float32)
    attended, peaks, totals, middle, attended_full = kept_state
    token_rows, model_width = stream.shape
    normed, normal, inverse, query_flat, key_rows, values = project_inputs(
        stream, gathered, layer_index, head_count
    )
    normed_two, normal_two, inverse_two, hidden = feed_inputs(middle, gathered, layer_index)
    active = gelu_tanh(hidden).astype(jnp.bfloat16)
    grad_branch = grad_stream.astype(jnp.bfloat16)
    grad_proj = outer_sum(active, grad_branch)
    grad_active = jnp.dot(grad_branch, w_proj[:, layer_index].T, preferred_element_type=jnp.float32)
    unused, gelu_pull = jax.vjp(gelu_tanh, hidden)
    grad_hidden = gelu_pull(grad_active)[0].astype(jnp.bfloat16)
    grad_fc = outer_sum(normed_two, grad_hidden)
    grad_normed_two = jnp.dot(
        grad_hidden, w_fc[:, layer_index].T, preferred_element_type=jnp.float32
    )
    grad_middle = grad_stream + norm_backward(
        grad_normed_two, normal_two, inverse_two, gains[:, 2 * layer_index + 1]
    )
    gain_two = jnp.sum(grad_normed_two * normal_two, axis=0)
    bias_two = jnp.sum(grad_normed_two, axis=0)
    grad_middle_low = grad_middle.astype(jnp.bfloat16)
    grad_out = outer_sum(attended, grad_middle_low)
    grad_attended = jnp.dot(
        grad_middle_low, w_out[:, layer_index].T, preferred_element_type=jnp.float32
    ).astype(jnp.bfloat16)
    query_all, grad_all = (
        lax.all_gather(query_flat, "ka", axis=0, tiled=True),
        lax.all_gather(grad_attended, "ka", axis=0, tiled=True),
    )
    query_all = query_all.reshape(query_all.shape[0], head_count, -1)
    grad_all = grad_all.reshape(grad_all.shape[0], head_count, -1)
    grad_keys, grad_values, grad_partials = attend_backward(
        query_all, grad_all, key_rows, values, peaks, totals, context, layer_index == 0
    )
    grad_queries = lax.psum_scatter(
        grad_partials.astype(jnp.bfloat16), "ka", scatter_dimension=0, tiled=True
    )
    grad_projected = jnp.concatenate(
        [
            grad_queries,
            grad_keys.reshape(token_rows, -1).astype(jnp.bfloat16),
            grad_values.reshape(token_rows, -1).astype(jnp.bfloat16),
        ],
        axis=1,
    )
    grad_qkv = outer_sum(normed, grad_projected)
    grad_normed = jnp.dot(
        grad_projected, w_qkv[:, layer_index].T, preferred_element_type=jnp.float32
    )
    grad_input = grad_middle + norm_backward(
        grad_normed, normal, inverse, gains[:, 2 * layer_index]
    )
    gain_one = jnp.sum(grad_normed * normal, axis=0)
    bias_one = jnp.sum(grad_normed, axis=0)
    gain_pair = jnp.stack([gain_one, gain_two], axis=1)
    bias_pair = jnp.stack([bias_one, bias_two], axis=1)
    return (grad_input, (grad_qkv, grad_out, grad_fc, grad_proj, gain_pair, bias_pair))


def on_device(
    tokens, cotangent, lengths, keep_mask, w_qkv, w_out, w_fc, w_proj, norm_gain, norm_bias
):
    token_rows = tokens.shape[0]
    head_count = H
    members = lax.axis_size("ka")
    group_rows = token_rows * members
    key_rank = lax.axis_index("ka")
    key_place = key_rank * token_rows + jnp.arange(token_rows, dtype=jnp.int32)
    bounds = jnp.cumsum(lengths[0])
    places = jnp.arange(group_rows, dtype=jnp.int32)
    segment_all = jnp.sum((places[:, None] >= bounds[None, :]).astype(jnp.int32), axis=1)
    segment_keys = lax.dynamic_slice_in_dim(segment_all, key_rank * token_rows, token_rows, 0)
    context = (segment_all, segment_keys, key_place, keep_mask > 0)
    gathered = (
        lax.all_gather(w_qkv, "pb", axis=0, tiled=True),
        lax.all_gather(w_out, "pb", axis=0, tiled=True),
        lax.all_gather(w_fc, "pb", axis=0, tiled=True),
        lax.all_gather(w_proj, "pb", axis=0, tiled=True),
        lax.all_gather(norm_gain, "pb", axis=0, tiled=True),
        lax.all_gather(norm_bias, "pb", axis=0, tiled=True),
    )
    stream = tokens.astype(jnp.float32)
    inputs = []
    states = []
    for layer_index in range(2):
        inputs.append(stream)
        stream, kept_state = layer_forward(stream, gathered, layer_index, context, head_count)
        states.append(kept_state)
    output = stream.astype(jnp.bfloat16)
    gathered = (
        lax.all_gather(w_qkv, "pb", axis=0, tiled=True),
        lax.all_gather(w_out, "pb", axis=0, tiled=True),
        lax.all_gather(w_fc, "pb", axis=0, tiled=True),
        lax.all_gather(w_proj, "pb", axis=0, tiled=True),
        lax.all_gather(norm_gain, "pb", axis=0, tiled=True),
        lax.all_gather(norm_bias, "pb", axis=0, tiled=True),
    )
    grad_stream = cotangent.astype(jnp.float32)
    pieces = [None, None]
    for layer_index in (1, 0):
        grad_stream, gradients = layer_backward(
            grad_stream,
            inputs[layer_index],
            states[layer_index],
            gathered,
            layer_index,
            context,
            head_count,
        )
        pieces[layer_index] = gradients
    stacked = tuple(
        (jnp.stack([pieces[0][member], pieces[1][member]], axis=1) for member in range(4))
    )
    gain_grads = jnp.concatenate([pieces[0][4], pieces[1][4]], axis=1)
    bias_grads = jnp.concatenate([pieces[0][5], pieces[1][5]], axis=1)
    stacked_qkv, stacked_out, stacked_fc, stacked_proj, gain_grads, bias_grads = (
        lax.psum_scatter(stacked[0], ("pb", "ka"), scatter_dimension=0, tiled=True),
        lax.psum_scatter(stacked[1], ("pb", "ka"), scatter_dimension=0, tiled=True),
        lax.psum_scatter(stacked[2], ("pb", "ka"), scatter_dimension=0, tiled=True),
        lax.psum_scatter(stacked[3], ("pb", "ka"), scatter_dimension=0, tiled=True),
        lax.psum_scatter(gain_grads, ("pb", "ka"), scatter_dimension=0, tiled=True),
        lax.psum_scatter(bias_grads, ("pb", "ka"), scatter_dimension=0, tiled=True),
    )
    summed = (
        lax.all_gather(stacked_qkv.astype(jnp.bfloat16), "ka", axis=0, tiled=True).astype(
            stacked_qkv.dtype
        ),
        lax.all_gather(stacked_out.astype(jnp.bfloat16), "ka", axis=0, tiled=True).astype(
            stacked_out.dtype
        ),
        lax.all_gather(stacked_fc.astype(jnp.bfloat16), "ka", axis=0, tiled=True).astype(
            stacked_fc.dtype
        ),
        lax.all_gather(stacked_proj.astype(jnp.bfloat16), "ka", axis=0, tiled=True).astype(
            stacked_proj.dtype
        ),
        lax.all_gather(gain_grads.astype(jnp.bfloat16), "ka", axis=0, tiled=True).astype(
            gain_grads.dtype
        ),
        lax.all_gather(bias_grads.astype(jnp.bfloat16), "ka", axis=0, tiled=True).astype(
            bias_grads.dtype
        ),
    )
    return (output, grad_stream, summed[0], summed[1], summed[2], summed[3], summed[4], summed[5])


def solution(mesh):
    return jax.shard_map(
        on_device,
        mesh=mesh,
        in_specs=(
            P(("pb", "ka"), None),
            P(("pb", "ka"), None),
            P("pb", None),
            P(("pb", "ka")),
            P("pb", None, None),
            P("pb", None, None),
            P("pb", None, None),
            P("pb", None, None),
            P("pb", None),
            P("pb", None),
        ),
        out_specs=(
            P(("pb", "ka"), None),
            P(("pb", "ka"), None),
            P("pb", None, None),
            P("pb", None, None),
            P("pb", None, None),
            P("pb", None, None),
            P("pb", None),
            P("pb", None),
        ),
        check_vma=False,
    )
```

profile of v0, /device:TPU:0, one launch (start us, length us, event | category | flops | bytes accessed | tf_op | source)
XLA Modules:
  0.0 1453.9 jit_solution(7139992192021137883)
XLA Ops:
  11.4 22.5 %all-gather.5 = bf16[8,96,4]{1,2,0:T(4,128)(2,1)S(1)} all-gather(bf16[1,96,4]{1,2,0:T(4,128)(2,1)S(1)} %bitcast.238), channel_id=1, replica_groups=mesh['pb'=8,'ka'=4] {'pb'}, dimensions={0}, use_global_device_ids=true | all-gather | bytes 6912 | tf_op jit(solution)/shard_map/all_gather | solution.py:302
  33.9 16.5 %all-gather.4 = bf16[8,96,4]{1,2,0:T(4,128)(2,1)S(1)} all-gather(bf16[1,96,4]{1,2,0:T(4,128)(2,1)S(1)} %bitcast.239), channel_id=1, replica_groups=mesh['pb'=8,'ka'=4] {'pb'}, dimensions={0}, use_global_device_ids=true | all-gather | bytes 6912 | tf_op jit(solution)/shard_map/all_gather | solution.py:301
  52.1 70.4 %all-gather.19.cloned.1.call-done = bf16[768,2,2304]{2,0,1:T(8,128)(2,1)} async-done(((bf16[96,2,2304]{2,0,1:T(8,128)(2,1)}), bf16[768,2,2304]{2,0,1:T(8,128)(2,1)}) %all-gather.19.cloned.1.call-update) | async-done | bytes 7077904 | tf_op jit(solution)/shard_map/all_gather | solution.py:297
  126.1 8.6 all_gather.83
  165.6 9.8 all-gather.21.cloned.1.call-done
  175.4 24.9 %reduce-scatter.27.cloned.1.call-done = bf16[128,768]{1,0:T(8,128)(2,1)} async-done(((bf16[512,768]{1,0:T(8,128)(2,1)}), bf16[128,768]{1,0:T(8,128)(2,1)}) %reduce-scatter.27.cloned.1.call-update) | async-done | bytes 196624
  203.4 137.9 %all-gather.23.cloned.1.call-done = bf16[768,2,3072]{2,0,1:T(8,128)(2,1)} async-done(((bf16[96,2,3072]{2,0,1:T(8,128)(2,1)}), bf16[768,2,3072]{2,0,1:T(8,128)(2,1)}) %all-gather.23.cloned.1.call-update) | async-done | bytes 9437200 | tf_op jit(solution)/shard_map/all_gather | solution.py:299
  345.7 134.7 %all-gather.25.cloned.1.call-done = bf16[3072,2,768]{2,0,1:T(8,128)(2,1)} async-done(((bf16[384,2,768]{2,0,1:T(8,128)(2,1)}), bf16[3072,2,768]{2,0,1:T(8,128)(2,1)}) %all-gather.25.cloned.1.call-update) | async-done | bytes 9437200 | tf_op jit(solution)/shard_map/all_gather | solution.py:300
  489.9 10.2 all_gather.89
  529.8 21.2 %reduce-scatter.29.cloned.1.call-done = bf16[128,768]{1,0:T(8,128)(2,1)} async-done(((bf16[512,768]{1,0:T(8,128)(2,1)}), bf16[128,768]{1,0:T(8,128)(2,1)}) %reduce-scatter.29.cloned.1.call-update) | async-done | bytes 196624
  565.9 8.7 all_gather.92
  582.5 12.2 psum.16
  610.4 16.9 %reduce-scatter.31.cloned.1.call-done = bf16[128,768]{1,0:T(8,128)(2,1)} async-done(((bf16[512,768]{1,0:T(8,128)(2,1)}), bf16[128,768]{1,0:T(8,128)(2,1)}) %reduce-scatter.31.cloned.1.call-update) | async-done | bytes 196624
  642.2 8.6 all_gather.93
  657.2 12.2 psum.17
  683.6 7.2 pad_maximum_fusion
  722.3 13.1 pad_maximum_fusion.2
  735.7 178.7 %reduce-scatter.23.cloned.1.call-done = f32[24,2,3072]{2,0,1:T(8,128)} async-done(((f32[768,2,3072]{2,0,1:T(8,128)}), f32[24,2,3072]{2,0,1:T(8,128)}) %reduce-scatter.23.cloned.1.call-update) | async-done | bytes 589840 | tf_op jit(solution)/shard_map/reduce_scatter | solution.py:341
  920.6 204.1 %reduce-scatter.25.cloned.1.call-done = f32[96,2,768]{2,0,1:T(8,128)} async-done(((f32[3072,2,768]{2,0,1:T(8,128)}), f32[96,2,768]{2,0,1:T(8,128)}) %reduce-scatter.25.cloned.1.call-update) | async-done | bytes 589840 | tf_op jit(solution)/shard_map/reduce_scatter | solution.py:342
  1130.2 39.5 %all-reduce.2 = (bf16[768,4]{0,1:T(4,128)(2,1)S(1)}, bf16[768,4]{0,1:T(4,128)(2,1)S(1)}) all-reduce(f32[768,4]{0,1:T(4,128)S(1)} %pad_maximum_fusion.10, f32[768,4]{0,1:T(4,128)S(1)} %pad_maximum_fusion.11), channel_id=14, replica_groups=mesh['pb'=8,'ka'=4] {'pb','ka'}, use_global_device_ids=true, to_apply=%region_42.43.clone | all-reduce | flops 6144 | bytes 36864
  1182.7 53.4 %reduce-scatter.21.cloned.1.call-done = f32[24,2,768]{2,0,1:T(8,128)} async-done(((f32[768,2,768]{2,0,1:T(8,128)}), f32[24,2,768]{2,0,1:T(8,128)}) %reduce-scatter.21.cloned.1.call-update) | async-done | bytes 147472 | tf_op jit(solution)/shard_map/reduce_scatter | solution.py:340
  1244.1 160.8 %reduce-scatter.19.cloned.1.call-done = f32[24,2,2304]{2,0,1:T(8,128)} async-done(((f32[768,2,2304]{2,0,1:T(8,128)}), f32[24,2,2304]{2,0,1:T(8,128)}) %reduce-scatter.19.cloned.1.call-update) | async-done | bytes 442384 | tf_op jit(solution)/shard_map/reduce_scatter | solution.py:339
  1406.0 9.1 all_gather.94
  1427.4 15.7 %all-gather.29.cloned.1.call-done = bf16[384,2,768]{2,0,1:T(8,128)(2,1)} async-done(((bf16[96,2,768]{2,0,1:T(8,128)(2,1)}), bf16[384,2,768]{2,0,1:T(8,128)(2,1)}) %all-gather.29.cloned.1.call-update) | async-done | bytes 1179664 | tf_op jit(solution)/shard_map/all_gather | solution.py:356
  (341 shorter events, 247.8 us)
Async XLA Ops:
  7.2 115.3 %all-gather.19.cloned.1.call-start = ((), (), s32[]{:S(2)}) async-start(), calls=%async_computation.8 | async-start | bytes 7962624 | tf_op jit(solution)/shard_map/all_gather | solution.py:297
  9.5 165.9 %all-gather.21.cloned.1.call-start = ((), (), s32[]{:S(2)}) async-start(), calls=%async_computation.9 | async-start | bytes 2654208 | tf_op jit(solution)/shard_map/all_gather | solution.py:298
  11.3 189.0 %reduce-scatter.27.cloned.1.call-start = ((), (), s32[]{:S(2)}) async-start(), calls=%async_computation.18 | async-start | bytes 983040
  50.6 74.6 %copy-start.50 = (f32[128]{0:T(128)}, f32[128]{0:T(128)S(1)}, u32[]{:S(2)}) copy-start(f32[128]{0:T(128)S(1)} %broadcast_multiply_fusion.11) | copy-start | bytes 1540
  50.9 74.4 %copy-start.59 = (f32[128]{0:T(128)}, f32[128]{0:T(128)S(1)}, u32[]{:S(2)}) copy-start(f32[128]{0:T(128)S(1)} %add_rsqrt_fusion.3) | copy-start | bytes 1540
  52.0 101.1 %copy-start.18 = (f32[512,128]{0,1:T(8,128)}, f32[512,128]{0,1:T(8,128)S(1)}, u32[]{:S(2)}) copy-start(f32[512,128]{0,1:T(8,128)S(1)} %get-tuple-element.538) | copy-start | bytes 786436
  52.1 101.1 %copy-start.24 = (pred[512,128]{0,1:T(8,128)(4,1)}, pred[512,128]{0,1:T(8,128)(4,1)S(1)}, u32[]{:S(2)}) copy-start(pred[512,128]{0,1:T(8,128)(4,1)S(1)} %get-tuple-element.539) | copy-start | bytes 196612
  160.4 180.8 %all-gather.23.cloned.1.call-start = ((), (), s32[]{:S(2)}) async-start(), calls=%async_computation.10 | async-start | bytes 10616832 | tf_op jit(solution)/shard_map/all_gather | solution.py:299
  163.0 317.4 %all-gather.25.cloned.1.call-start = ((), (), s32[]{:S(2)}) async-start(), calls=%async_computation.11 | async-start | bytes 10616832 | tf_op jit(solution)/shard_map/all_gather | solution.py:300
  165.5 385.5 %reduce-scatter.29.cloned.1.call-start = ((), (), s32[]{:S(2)}) async-start(), calls=%async_computation.19 | async-start | bytes 983040
  202.1 143.6 %copy-start.15 = (f32[128,768]{1,0:T(8,128)}, f32[128,768]{1,0:T(8,128)S(1)}, u32[]{:S(2)}) copy-start(f32[128,768]{1,0:T(8,128)S(1)} %get-tuple-element.543) | copy-start | bytes 1179652
  529.8 97.6 %reduce-scatter.31.cloned.1.call-start = ((), (), s32[]{:S(2)}) async-start(), calls=%async_computation.20 | async-start | bytes 983040
  603.4 112.5 %reduce-scatter.33.cloned.1.call-start = ((), (), s32[]{:S(2)}) async-start(), calls=%async_computation.21 | async-start | bytes 983040
  678.9 235.5 %reduce-scatter.23.cloned.1.call-start = ((), (), s32[]{:S(2)}) async-start(), calls=%async_computation.14 | async-start | bytes 19464192 | tf_op jit(solution)/shard_map/reduce_scatter | solution.py:341
  690.8 434.0 %reduce-scatter.25.cloned.1.call-start = ((), (), s32[]{:S(2)}) async-start(), calls=%async_computation.16 | async-start | bytes 19464192 | tf_op jit(solution)/shard_map/reduce_scatter | solution.py:342
  702.3 533.9 %reduce-scatter.21.cloned.1.call-start = ((), (), s32[]{:S(2)}) async-start(), calls=%async_computation.13 | async-start | bytes 4866048 | tf_op jit(solution)/shard_map/reduce_scatter | solution.py:340
  707.9 697.0 %reduce-scatter.19.cloned.1.call-start = ((), (), s32[]{:S(2)}) async-start(), calls=%async_computation.12 | async-start | bytes 14598144 | tf_op jit(solution)/shard_map/reduce_scatter | solution.py:339
  735.4 180.9 %copy-start.67 = (f32[768]{0:T(1024)S(1)}, f32[768]{0:T(1024)}, u32[]{:S(2)}) copy-start(f32[768]{0:T(1024)} %get-tuple-element.486) | copy-start | bytes 9220
  735.4 180.9 %copy-start.66 = (f32[768]{0:T(1024)S(1)}, f32[768]{0:T(1024)}, u32[]{:S(2)}) copy-start(f32[768]{0:T(1024)} %get-tuple-element.497) | copy-start | bytes 9220
  735.4 181.0 %copy-start.6 = (f32[128,768]{1,0:T(8,128)S(1)}, f32[128,768]{1,0:T(8,128)}, u32[]{:S(2)}) copy-start(f32[128,768]{1,0:T(8,128)} %copy-done.5) | copy-start | bytes 1179652
  735.4 181.0 %copy-start.29 = (f32[128,3072]{1,0:T(8,128)S(1)}, f32[128,3072]{1,0:T(8,128)}, u32[]{:S(2)}) copy-start(f32[128,3072]{1,0:T(8,128)} %copy-done.28) | copy-start | bytes 4718596
  735.4 688.1 %all-gather.27.cloned.1.call-start = ((), (), s32[]{:S(2)}) async-start(), calls=%async_computation.15 | async-start | bytes 1474560 | tf_op jit(solution)/shard_map/all_gather | solution.py:353
  916.3 526.8 %all-gather.29.cloned.1.call-start = ((), (), s32[]{:S(2)}) async-start(), calls=%async_computation.17 | async-start | bytes 1474560 | tf_op jit(solution)/shard_map/all_gather | solution.py:356
  916.4 210.2 %copy-start.39 = (bf16[12,64,128]{2,1,0:T(8,128)(2,1)S(1)}, bf16[12,64,128]{2,1,0:T(8,128)(2,1)}, u32[]{:S(2)}) copy-start(bf16[12,64,128]{2,1,0:T(8,128)(2,1)} %fusion.36) | copy-start | bytes 589828
  (72 other events, 577.3 us)
Sparse Core Ops, SparseCore 0:
  10.8 111.6 all-gather.18
  125.2 50.1 all-gather.20
  178.5 21.7 reduce-scatter.26
  203.2 138.0 all-gather.22
  344.1 136.2 all-gather.24
  529.9 21.0 reduce-scatter.28
  603.5 23.7 reduce-scatter.30
  679.0 23.7 reduce-scatter.32
  709.3 205.1 reduce-scatter.22
  920.7 204.0 reduce-scatter.24
  1130.2 105.8 reduce-scatter.20
  1243.0 161.8 reduce-scatter.18
  1407.1 16.3 all-gather.26
  1425.6 17.4 all-gather.28
where the time goes:
time: 1460 us; the launch traced here: 1450 us
  waiting for transfers between devices  1040 us (71%)
  blocking collectives  186 us (13%)
  matrix products  99.9 us (7%)
  other arithmetic  60.3 us (4%)
  local copies, waits for them, and re-layouts  55.9 us (4%)
  between operations  15.6 us (1%)
    reduce_scatter x1, waiting for transfers between devices, on_device(): lax.psum_scatter(stacked[3], ('pb', 'ka'), scatter_dimension=0, tiled=True)  204 us
    reduce_scatter x1, waiting for transfers between devices, on_device(): lax.psum_scatter(stacked[2], ('pb', 'ka'), scatter_dimension=0, tiled=True)  179 us
    reduce_scatter x1, waiting for transfers between devices, on_device(): lax.psum_scatter(stacked[0], ('pb', 'ka'), scatter_dimension=0, tiled=True)  161 us
    all_gather x1, waiting for transfers between devices, on_device(): lax.all_gather(w_fc, 'pb', axis=0, tiled=True)  138 us
    all_gather x1, waiting for transfers between devices, on_device(): lax.all_gather(w_proj, 'pb', axis=0, tiled=True)  135 us
    all_gather x1, waiting for transfers between devices, on_device(): lax.all_gather(w_qkv, 'pb', axis=0, tiled=True)  70.4 us
    unnamed x18, waiting for transfers between devices  63.3 us
    reduce_scatter x1, waiting for transfers between devices, on_device(): lax.psum_scatter(stacked[1], ('pb', 'ka'), scatter_dimension=0, tiled=True)  53.4 us
  transfers between devices with their start and end apart: 14, of which 13 were waited for; matrix products, arithmetic and copies ran while one was open for 8% of the time, Pallas kernels for 0%

commit v1 on v0

v1 whole, which is shorter than its diff:
```python
import jax
import jax.numpy as jnp
from jax import lax
from jax.sharding import PartitionSpec as P

H = 12
EPSILON = 1e-05
FLOOR_VALUE = -1e30
BF = jnp.bfloat16
F32 = jnp.float32


def dot(a, b, ca, cb):
    return lax.dot_general(a, b, (((ca,), (cb,)), ((), ())), preferred_element_type=F32)


def norm_forward(values, gain_row, offset):
    average = jnp.mean(values, axis=-1, keepdims=True)
    centered = values - average
    spread = jnp.mean(centered * centered, axis=-1, keepdims=True)
    inverse = lax.rsqrt(spread + EPSILON)
    normal = centered * inverse
    return (normal * gain_row + offset, normal, inverse)


def norm_backward(grad_out, normal, inverse, gain_row):
    grad_normal = grad_out * gain_row
    mean_grad = jnp.mean(grad_normal, axis=-1, keepdims=True)
    mean_cross = jnp.mean(grad_normal * normal, axis=-1, keepdims=True)
    return inverse * (grad_normal - mean_grad - normal * mean_cross)


def gelu_tanh(v):
    return jax.nn.gelu(v, approximate=True)


def swap(x, axis, bit):
    size = lax.axis_size(axis)
    return lax.ppermute(x, axis, [(i, i ^ bit) for i in range(size)])


class Halves:
    def __init__(self):
        self.me = lax.axis_index("ka")
        self.low = self.me % 2
        self.high = self.me // 2

    def take(self, full, low):
        rows = full.shape[0] // 4
        parts = full.reshape((2, 2, rows) + full.shape[1:])
        return lax.dynamic_index_in_dim(parts, low, 1, False).reshape((2 * rows,) + full.shape[1:])

    def join(self, own, other):
        rows = own.shape[0] // 2
        own = own.reshape((2, 1, rows) + own.shape[1:])
        other = other.reshape((2, 1, rows) + other.shape[1:])
        first = jnp.where(self.low == 0, own, other)
        second = jnp.where(self.low == 0, other, own)
        return jnp.concatenate([first, second], axis=1).reshape((4 * rows,) + own.shape[3:])

    def own_block(self, half):
        rows = half.shape[0] // 2
        return lax.dynamic_slice_in_dim(half, self.high * rows, rows, 0)

    def spread(self, half):
        return self.join(half, swap(half, "ka", 1))

    def reduce(self, partial):
        kept = self.take(partial, self.low)
        sent = self.take(partial, 1 - self.low).astype(BF)
        pair = (kept + swap(sent, "ka", 1).astype(F32)).astype(BF)
        return pair.astype(F32) + swap(pair, "ka", 2).astype(F32)


def attention_scores(q, k, allowed, signed, scale):
    scores = jnp.einsum("qhd,khd->hqk", q, k, preferred_element_type=F32) * scale
    magnitude = jnp.abs(scores) if signed else scores
    return scores, jnp.where(allowed[None], magnitude, FLOOR_VALUE)


def attend_forward(q, k, v, allowed, signed):
    scale = q.shape[2] ** (-0.5)
    scores, masked = attention_scores(q, k, allowed, signed, scale)
    peak = jnp.max(masked, axis=-1, keepdims=True)
    raised = jnp.exp(masked - peak)
    total = jnp.sum(raised, axis=-1, keepdims=True)
    if signed:
        numerator = jnp.sign(scores) * (raised - jnp.exp(-peak) * allowed[None].astype(F32))
    else:
        numerator = raised
    weights_low = (numerator / total).astype(BF)
    out = jnp.einsum("hqk,khd->qhd", weights_low, v, preferred_element_type=F32)
    return out.astype(BF), peak, total


def attend_backward(q, k, v, grad, peak, total, allowed, signed):
    scale = q.shape[2] ** (-0.5)
    scores, masked = attention_scores(q, k, allowed, signed, scale)
    raised = jnp.exp(masked - peak)
    absolute = raised / total
    if signed:
        signs = jnp.sign(scores)
        weights = signs * (raised - jnp.exp(-peak) * allowed[None].astype(F32)) / total
    else:
        signs = 1.0
        weights = absolute
    grad_weights = jnp.einsum("qhd,khd->hqk", grad, v, preferred_element_type=F32)
    delta = jnp.sum(grad_weights * weights, axis=-1, keepdims=True)
    grad_scores = (absolute * (grad_weights - signs * delta)).astype(BF)
    gq = jnp.einsum("hqk,khd->qhd", grad_scores, k, preferred_element_type=F32) * scale
    gk = jnp.einsum("hqk,qhd->khd", grad_scores, q, preferred_element_type=F32) * scale
    gv = jnp.einsum("hqk,qhd->khd", weights.astype(BF), grad, preferred_element_type=F32)
    return gq.astype(BF), gk.astype(BF), gv.astype(BF)


def gather_rows(x):
    return lax.all_gather(x, "pb", axis=0, tiled=True)


def scatter_rows(x):
    return lax.psum_scatter(x.astype(BF), "pb", scatter_dimension=0, tiled=True).astype(F32)


def row_moves(pb, ka):
    span = pb // ka
    forward = []
    for p in range(pb):
        for k in range(ka):
            forward.append((p * ka + k, ((p % span) * ka + k) * ka + p // span))
    return forward


def on_device(tokens, cotangent, lengths, keep_mask, w_qkv, w_out, w_fc, w_proj, norm_gain, norm_bias):
    rows, width = tokens.shape
    pb = lax.axis_size("pb")
    ka = lax.axis_size("ka")
    me = lax.axis_index("ka")
    halves = Halves()
    group = rows * ka
    heads = H // ka
    part = width // ka
    hd = width // H
    ff = w_fc.shape[2]
    ff_part = ff // ka

    local_qkv = lax.dynamic_index_in_dim(w_qkv.reshape(w_qkv.shape[0], 2, 3, ka, part), me, 3, False)
    local_qkv = local_qkv.reshape(w_qkv.shape[0], 2, 3 * part)
    local_fc = lax.dynamic_slice_in_dim(w_fc, me * ff_part, ff_part, 2)
    out_rows = w_out.shape[0] // ka
    proj_rows = w_proj.shape[0] // ka
    moves = row_moves(pb, ka)
    tall = jnp.concatenate(
        [
            lax.dynamic_slice_in_dim(w_out, me * out_rows, out_rows, 0),
            lax.dynamic_slice_in_dim(w_proj, me * proj_rows, proj_rows, 0),
        ],
        axis=0,
    )
    tall = lax.ppermute(tall, ("pb", "ka"), moves)
    gains = gather_rows(norm_gain).astype(F32)
    offsets = gather_rows(norm_bias).astype(F32)
    qkv, out, fc, proj = [], [], [], []
    for l in range(2):
        qkv.append(gather_rows(local_qkv[:, l]))
        out.append(gather_rows(tall[:out_rows, l]))
        fc.append(gather_rows(local_fc[:, l]))
        proj.append(gather_rows(tall[out_rows:, l]))

    places = jnp.arange(group, dtype=jnp.int32)
    bounds = jnp.cumsum(lengths[0])
    segment = jnp.sum((places[:, None] >= bounds[None, :]).astype(jnp.int32), axis=1)
    kept = lax.all_gather(keep_mask, "ka", axis=0, tiled=True) > 0
    allowed = (segment[:, None] == segment[None, :]) & (places[None, :] <= places[:, None])
    allowed = allowed & (kept[None, :] | (places[None, :] == places[:, None]))

    tokens_all = lax.all_gather(tokens, "ka", axis=0, tiled=True)
    cotangent_all = lax.all_gather(cotangent, "ka", axis=0, tiled=True)

    def split(projected):
        return [projected[:, i * part : (i + 1) * part].reshape(group, heads, hd) for i in range(3)]

    stream = halves.take(tokens_all, halves.low).astype(F32)
    saved = []
    for l in range(2):
        normed, normal, inverse = norm_forward(stream, gains[:, 2 * l], offsets[:, 2 * l])
        normed_all = halves.spread(normed.astype(BF))
        projected = dot(normed_all, qkv[l], 1, 0).astype(BF)
        q, k, v = split(projected)
        attended, peak, total = attend_forward(q, k, v, allowed, l == 0)
        attended = attended.reshape(group, part)
        middle = stream + halves.reduce(dot(attended, out[l], 1, 0))
        normed_two, normal_two, inverse_two = norm_forward(middle, gains[:, 2 * l + 1], offsets[:, 2 * l + 1])
        normed_two_all = halves.spread(normed_two.astype(BF))
        hidden = dot(normed_two_all, fc[l], 1, 0)
        active = gelu_tanh(hidden).astype(BF)
        stream = middle + halves.reduce(dot(active, proj[l], 1, 0))
        saved.append((normed_all, normal, inverse, projected, attended, peak, total, normed_two_all, normal_two, inverse_two, hidden, active))
    output = halves.own_block(stream).astype(BF)

    grad_stream = halves.take(cotangent_all, halves.low).astype(F32)
    branch_all = cotangent_all
    grads = [None, None]
    for l in (1, 0):
        (normed_all, normal, inverse, projected, attended, peak, total, normed_two_all, normal_two, inverse_two, hidden, active) = saved[l]
        grad_active = dot(branch_all, proj[l], 1, 1)
        grad_proj = dot(active, branch_all, 0, 0)
        unused, pull = jax.vjp(gelu_tanh, hidden)
        grad_hidden = pull(grad_active)[0].astype(BF)
        grad_fc = dot(normed_two_all, grad_hidden, 0, 0)
        grad_normed_two = halves.reduce(dot(grad_hidden, fc[l], 1, 1))
        grad_middle = grad_stream + norm_backward(grad_normed_two, normal_two, inverse_two, gains[:, 2 * l + 1])
        gain_two = jnp.sum(halves.own_block(grad_normed_two * normal_two), axis=0)
        bias_two = jnp.sum(halves.own_block(grad_normed_two), axis=0)
        middle_all = halves.spread(grad_middle.astype(BF))
        grad_out = dot(attended, middle_all, 0, 0)
        grad_attended = dot(middle_all, out[l], 1, 1).astype(BF).reshape(group, heads, hd)
        q, k, v = split(projected)
        gq, gk, gv = attend_backward(q, k, v, grad_attended, peak, total, allowed, l == 0)
        grad_projected = jnp.concatenate([g.reshape(group, part) for g in (gq, gk, gv)], axis=1)
        grad_qkv = dot(normed_all, grad_projected, 0, 0)
        grad_normed = halves.reduce(dot(grad_projected, qkv[l], 1, 1))
        grad_stream = grad_middle + norm_backward(grad_normed, normal, inverse, gains[:, 2 * l])
        gain_one = jnp.sum(halves.own_block(grad_normed * normal), axis=0)
        bias_one = jnp.sum(halves.own_block(grad_normed), axis=0)
        if l:
            branch_all = halves.spread(grad_stream.astype(BF))
        grads[l] = (grad_qkv, grad_out, grad_fc, grad_proj, gain_one, gain_two, bias_one, bias_two)
    grad_tokens = halves.own_block(grad_stream)

    vectors = jnp.stack([grads[0][4], grads[0][5], grads[1][4], grads[1][5], grads[0][6], grads[0][7], grads[1][6], grads[1][7]], axis=1)
    vectors = lax.psum(vectors, ("pb", "ka"))
    vectors = lax.dynamic_slice_in_dim(vectors, lax.axis_index("pb") * norm_gain.shape[0], norm_gain.shape[0], 0)
    back = [(b, a) for a, b in moves]
    pieces = []
    for l in range(2):
        qkv_part = scatter_rows(grads[l][0]).astype(BF)
        out_part = scatter_rows(grads[l][1]).astype(BF)
        fc_part = scatter_rows(grads[l][2]).astype(BF)
        proj_part = scatter_rows(grads[l][3]).astype(BF)
        tall = lax.ppermute(jnp.concatenate([out_part, proj_part], axis=0), ("pb", "ka"), back)
        qkv_all = lax.all_gather(qkv_part.reshape(-1, 3, part), "ka", axis=2).reshape(-1, 3 * width)
        fc_all = lax.all_gather(fc_part, "ka", axis=1).reshape(-1, ff)
        tall = lax.all_gather(tall, "ka", axis=0)
        out_all = tall[:, :out_rows].reshape(-1, width)
        proj_all = tall[:, out_rows:].reshape(-1, width)
        pieces.append((qkv_all, out_all, fc_all, proj_all))
    summed = [jnp.stack([a, b], axis=1).astype(F32) for a, b in zip(*pieces)]
    return (output, grad_tokens, *summed, vectors[:, :4], vectors[:, 4:])


def solution(mesh):
    return jax.shard_map(
        on_device,
        mesh=mesh,
        in_specs=(
            P(("pb", "ka"), None),
            P(("pb", "ka"), None),
            P("pb", None),
            P(("pb", "ka")),
            P("pb", None, None),
            P("pb", None, None),
            P("pb", None, None),
            P("pb", None, None),
            P("pb", None),
            P("pb", None),
        ),
        out_specs=(
            P(("pb", "ka"), None),
            P(("pb", "ka"), None),
            P("pb", None, None),
            P("pb", None, None),
            P("pb", None, None),
            P("pb", None, None),
            P("pb", None),
            P("pb", None),
        ),
        check_vma=False,
    )
```

time: 1460 us -> 933 us (0.64)
  waiting for transfers between devices: 1040 us -> 424 us
  blocking collectives: 186 us -> 306 us
  matrix products: 99.9 us -> 67.8 us
  starting transfers between devices: 1.22 us -> 18.6 us
  other arithmetic: 60.3 us -> 45.2 us
    all_gather x6 -> x4, waiting for transfers between devices: 375 us -> 28.9 us  [gather_rows(): return lax.all_gather(x, 'pb', axis=0, tiled=True)]
    reduce_scatter x4 -> x8, waiting for transfers between devices: 597 us -> 318 us  [scatter_rows(): lax.psum_scatter(x.astype(BF), 'pb', scatter_dimension=0, tiled=True)]
    all_gather x14 -> x15, blocking collectives: 122 us -> 266 us  [the longest x6 187 us: gather_rows(): return lax.all_gather(x, 'pb', axis=0, tiled=True)]
    ppermute x0 -> x26, waiting for transfers between devices: none -> 77.1 us  [the longest x23 77.1 us: swap(): return lax.ppermute(x, axis, [(i, i ^ bit) for i in range(size)])]
    unnamed x18 -> x12, waiting for transfers between devices: 63.3 us -> 0.2 us
    dot_general x36 -> x34, matrix products: 99.9 us -> 57.8 us  [the longest x24 46.7 us: dot(): lax.dot_general(a, b, (((ca,), (cb,)), ((), ())), preferred_element_type=...]
    unnamed x1 -> x0, blocking collectives: 39.5 us -> none
    another operation x5 -> x1, other arithmetic: 29.6 us -> 0.18 us  [the longest x4 29.4 us: on_device(): jnp.stack([pieces[0][member], pieces[1][member]], axis=1)]
  transfers between devices with their start and end apart: 14 -> 38, of which waited for: 13 -> 24; matrix products, arithmetic and copies ran while one was open for 8% -> 14% of each run, Pallas kernels for 0% -> 0%
where the time goes in v1:
time: 933 us; the launch traced here: 924 us
  waiting for transfers between devices  424 us (45%)
  blocking collectives  306 us (33%)
  matrix products  67.8 us (7%)
  local copies, waits for them, and re-layouts  45.5 us (5%)
  other arithmetic  45.2 us (5%)
  starting transfers between devices  18.6 us (2%)
  between operations  16.2 us (2%)
    reduce_scatter x8, waiting for transfers between devices, scatter_rows(): lax.psum_scatter(x.astype(BF), 'pb', scatter_dimension=0, tiled=True)  318 us
    all_gather x6, blocking collectives, gather_rows(): return lax.all_gather(x, 'pb', axis=0, tiled=True)  187 us
    ppermute x23, waiting for transfers between devices, swap(): return lax.ppermute(x, axis, [(i, i ^ bit) for i in range(size)])  77.1 us
    dot_general x24, matrix products, dot(): lax.dot_general(a, b, (((ca,), (cb,)), ((), ())), preferred_element_type=...  46.7 us
    psum x1, blocking collectives, on_device(): vectors = lax.psum(vectors, ('pb', 'ka'))  39.9 us
    all_gather x4, waiting for transfers between devices, gather_rows(): return lax.all_gather(x, 'pb', axis=0, tiled=True)  28.9 us
    unnamed x211, local copies, waits for them, and re-layouts  21.1 us
    all_gather x2, blocking collectives, on_device(): lax.all_gather(qkv_part.reshape(-1, 3, part), 'ka', axis=2)  19.6 us
  transfers between devices with their start and end apart: 38, of which 24 were waited for; matrix products, arithmetic and copies ran while one was open for 14% of the time, Pallas kernels for 0%

profile of v1, /device:TPU:0, one launch (start us, length us, event | category | flops | bytes accessed | tf_op | source)
XLA Modules:
  0.0 923.5 jit_solution(1655315909987413133)
XLA Ops:
  13.3 42.0 %all-gather.12 = bf16[8,96,4]{1,2,0:T(4,128)(2,1)S(1)} all-gather(bf16[1,96,4]{1,2,0:T(4,128)(2,1)S(1)} %bitcast.366), channel_id=1, replica_groups=mesh['pb'=8,'ka'=4] {'pb'}, dimensions={0}, use_global_device_ids=true | all-gather | bytes 6912 | tf_op jit(solution)/shard_map/all_gather | solution.py:117
  56.0 16.3 %all-gather.13 = bf16[8,96,4]{1,2,0:T(4,128)(2,1)S(1)} all-gather(bf16[1,96,4]{1,2,0:T(4,128)(2,1)S(1)} %bitcast.367), channel_id=1, replica_groups=mesh['pb'=8,'ka'=4] {'pb'}, dimensions={0}, use_global_device_ids=true | all-gather | bytes 6912 | tf_op jit(solution)/shard_map/all_gather | solution.py:117
  73.0 11.6 %all_gather.69 = bf16[512,768]{1,0:T(8,128)(2,1)S(1)} all-gather(bf16[128,768]{1,0:T(8,128)(2,1)S(1)} %copy-done.57), channel_id=1, replica_groups=mesh['pb'=8,'ka'=4] {'ka'}, dimensions={0}, use_global_device_ids=true | all-gather | bytes 983040 | tf_op jit(solution)/shard_map/all_gather | solution.py:176
  95.2 32.6 %all-gather = bf16[768,1,576]{2,0,1:T(8,128)(2,1)S(1)} all-gather(bf16[96,1,576]{2,0,1:T(8,128)(2,1)S(1)} %copy.129), channel_id=2, replica_groups=mesh['pb'=8,'ka'=4] {'pb'}, dimensions={0}, use_global_device_ids=true | all-gather | bytes 995328 | tf_op jit(solution)/shard_map/all_gather | solution.py:117
  129.9 30.8 %all-gather.1 = bf16[192,1,768]{2,0,1:T(8,128)(2,1)S(1)} all-gather(bf16[24,1,768]{2,0,1:T(8,128)(2,1)S(1)} %get-tuple-element.121), channel_id=3, replica_groups=mesh['pb'=8,'ka'=4] {'pb'}, dimensions={0}, use_global_device_ids=true | all-gather | bytes 331776 | tf_op jit(solution)/shard_map/all_gather | solution.py:117
  176.2 10.0 %collective-permute-done.3 = bf16[256,768]{1,0:T(8,128)(2,1)} collective-permute-done((bf16[256,768]{1,0:T(8,128)(2,1)S(1)}, bf16[256,768]{1,0:T(8,128)(2,1)}, u32[]{:S(2)}, u32[]{:S(2)}) %collective-permute-start.3) | collective-permute-done | bytes 393248 | tf_op jit(solution)/shard_map/ppermute | solution.py:39
  197.4 17.3 %all-gather.22.cloned.1.call-done = bf16[768,1,768]{2,0,1:T(8,128)(2,1)} async-done(((bf16[96,1,768]{2,0,1:T(8,128)(2,1)}), bf16[768,1,768]{2,0,1:T(8,128)(2,1)}) %all-gather.22.cloned.1.call-update) | async-done | bytes 1179664 | tf_op jit(solution)/shard_map/all_gather | solution.py:117
  235.4 34.3 %all-gather.4 = bf16[768,1,576]{2,0,1:T(8,128)(2,1)S(1)} all-gather(bf16[96,1,576]{2,0,1:T(8,128)(2,1)S(1)} %copy-done.50), channel_id=6, replica_groups=mesh['pb'=8,'ka'=4] {'pb'}, dimensions={0}, use_global_device_ids=true | all-gather | bytes 995328 | tf_op jit(solution)/shard_map/all_gather | solution.py:117
  269.7 30.9 %all-gather.5 = bf16[192,1,768]{2,0,1:T(8,128)(2,1)S(1)} all-gather(bf16[24,1,768]{2,0,1:T(8,128)(2,1)S(1)} %copy-done.65), channel_id=7, replica_groups=mesh['pb'=8,'ka'=4] {'pb'}, dimensions={0}, use_global_device_ids=true | all-gather | bytes 331776 | tf_op jit(solution)/shard_map/all_gather | solution.py:117
  316.7 9.9 %collective-permute-done.9 = bf16[256,768]{1,0:T(8,128)(2,1)} collective-permute-done((bf16[256,768]{1,0:T(8,128)(2,1)}, bf16[256,768]{1,0:T(8,128)(2,1)}, u32[]{:S(2)}, u32[]{:S(2)}) %collective-permute-start.9) | collective-permute-done | bytes 393248 | tf_op jit(solution)/shard_map/ppermute | solution.py:39
  330.2 9.7 %all_gather.81 = bf16[512,768]{1,0:T(8,128)(2,1)} all-gather(bf16[128,768]{1,0:T(8,128)(2,1)S(1)} %copy-done.58), channel_id=1, replica_groups=mesh['pb'=8,'ka'=4] {'ka'}, dimensions={0}, use_global_device_ids=true | all-gather | bytes 983040 | tf_op jit(solution)/shard_map/all_gather | solution.py:177
  344.3 11.5 %all-gather.26.cloned.1.call-done = bf16[768,1,768]{2,0,1:T(8,128)(2,1)} async-done(((bf16[96,1,768]{2,0,1:T(8,128)(2,1)}), bf16[768,1,768]{2,0,1:T(8,128)(2,1)}) %all-gather.26.cloned.1.call-update) | async-done | bytes 1179664 | tf_op jit(solution)/shard_map/all_gather | solution.py:117
  363.8 9.7 %collective-permute-done.14 = bf16[256,768]{1,0:T(8,128)(2,1)S(1)} collective-permute-done((bf16[256,768]{1,0:T(8,128)(2,1)S(1)}, bf16[256,768]{1,0:T(8,128)(2,1)S(1)}, u32[]{:S(2)}, u32[]{:S(2)}) %collective-permute-start.14) | collective-permute-done | bytes 393248 | tf_op jit(solution)/shard_map/ppermute | solution.py:39
  394.2 9.9 %collective-permute-done.17 = bf16[256,768]{1,0:T(8,128)(2,1)S(1)} collective-permute-done((bf16[256,768]{1,0:T(8,128)(2,1)S(1)}, bf16[256,768]{1,0:T(8,128)(2,1)S(1)}, u32[]{:S(2)}, u32[]{:S(2)}) %collective-permute-start.17) | collective-permute-done | bytes 393248 | tf_op jit(solution)/shard_map/ppermute | solution.py:39
  457.9 50.8 %reduce-scatter.19.cloned.1.call-done = bf16[96,768]{1,0:T(8,128)(2,1)} async-done(((bf16[768,768]{1,0:T(8,128)(2,1)}), bf16[96,768]{1,0:T(8,128)(2,1)}) %reduce-scatter.19.cloned.1.call-update) | async-done | bytes 147472 | tf_op jit(solution)/shard_map/reduce_scatter | solution.py:121
  513.2 62.2 %reduce-scatter.23.cloned.1.call-done = bf16[96,768]{1,0:T(8,128)(2,1)} async-done(((bf16[768,768]{1,0:T(8,128)(2,1)}), bf16[96,768]{1,0:T(8,128)(2,1)}) %reduce-scatter.23.cloned.1.call-update) | async-done | bytes 147472 | tf_op jit(solution)/shard_map/reduce_scatter | solution.py:121
  600.8 8.5 all-gather.9
  609.4 31.8 %reduce-scatter.11.cloned.1.call-done = bf16[96,576]{1,0:T(8,128)(2,1)} async-done(((bf16[768,576]{1,0:T(8,128)(2,1)}), bf16[96,576]{1,0:T(8,128)(2,1)}) %reduce-scatter.11.cloned.1.call-update) | async-done | bytes 110608 | tf_op jit(solution)/shard_map/reduce_scatter | solution.py:121
  644.7 12.0 %all_gather.83 = bf16[96,3,4,192]{3,0,1,2:T(8,128)(2,1)S(1)} all-gather(bf16[96,3,1,192]{3,0,1,2:T(8,128)(2,1)S(1)} %copy.152), channel_id=1, replica_groups=mesh['pb'=8,'ka'=4] {'ka'}, dimensions={2}, use_global_device_ids=true | all-gather | bytes 552960 | tf_op jit(solution)/shard_map/all_gather | solution.py:241
  663.8 39.9 %psum.7 = f32[768,8]{0,1:T(8,128)S(1)} all-reduce(f32[768,8]{0,1:T(8,128)S(1)} %stack.51), channel_id=1, replica_groups=mesh['pb'=8,'ka'=4] {'pb','ka'}, use_global_device_ids=true, to_apply=%region_40.41 | all-reduce | flops 6144 | bytes 49152 | tf_op jit(solution)/shard_map/psum | solution.py:231
  704.4 65.5 %reduce-scatter.15.cloned.1.call-done = bf16[96,768]{1,0:T(8,128)(2,1)} async-done(((bf16[768,768]{1,0:T(8,128)(2,1)}), bf16[96,768]{1,0:T(8,128)(2,1)}) %reduce-scatter.15.cloned.1.call-update) | async-done | bytes 147472 | tf_op jit(solution)/shard_map/reduce_scatter | solution.py:121
  771.5 65.8 %reduce-scatter.21.cloned.1.call-done = bf16[96,768]{1,0:T(8,128)(2,1)} async-done(((bf16[768,768]{1,0:T(8,128)(2,1)}), bf16[96,768]{1,0:T(8,128)(2,1)}) %reduce-scatter.21.cloned.1.call-update) | async-done | bytes 147472 | tf_op jit(solution)/shard_map/reduce_scatter | solution.py:121
  848.4 8.7 all-gather.8
  861.8 42.0 %reduce-scatter.9.cloned.1.call-done = bf16[96,576]{1,0:T(8,128)(2,1)} async-done(((bf16[768,576]{1,0:T(8,128)(2,1)}), bf16[96,576]{1,0:T(8,128)(2,1)}) %reduce-scatter.9.cloned.1.call-update) | async-done | bytes 110608 | tf_op jit(solution)/shard_map/reduce_scatter | solution.py:121
  (466 shorter events, 243.6 us)
Async XLA Ops:
  7.2 186.8 %all-gather.20.cloned.1.call-start = ((), (), s32[]{:S(2)}) async-start(), calls=%async_computation.16 | async-start | bytes 1327104 | tf_op jit(solution)/shard_map/all_gather | solution.py:117
  9.5 119.6 %collective-permute-start.1 = (bf16[120,2,768]{2,0,1:T(8,128)(2,1)}, bf16[120,2,768]{2,0,1:T(8,128)(2,1)S(1)}, u32[]{:S(2)}, u32[]{:S(2)}) collective-permute-start(bf16[120,2,768]{2,0,1:T(8,128)(2,1)} %pad_maximum_fusion.9), channel_id=1, source_target_pairs={{0,0},{1,4},{2,8},{3,12},{4,16},{5,20},{6,24},{7,28},{8,1},{9,5},{... | collective-permute-start | bytes 1105928 | tf_op jit(solution)/shard_map/ppermute | solution.py:159
  13.2 201.6 %all-gather.22.cloned.1.call-start = ((), (), s32[]{:S(2)}) async-start(), calls=%async_computation.17 | async-start | bytes 1327104 | tf_op jit(solution)/shard_map/all_gather | solution.py:117
  86.3 74.4 %collective-permute-start = (bf16[256,768]{1,0:T(8,128)(2,1)}, bf16[256,768]{1,0:T(8,128)(2,1)}, u32[]{:S(2)}, u32[]{:S(2)}) collective-permute-start(bf16[256,768]{1,0:T(8,128)(2,1)} %get-tuple-element.94), channel_id=1, source_target_pairs={{0,1},{1,0},{2,3},{3,2},{4,5},{5,4},{6,7},{7,6},{8,9},{9,8},{10,11... | collective-permute-start | bytes 1179656 | tf_op jit(solution)/shard_map/ppermute | solution.py:39
  174.9 11.3 %collective-permute-start.3 = (bf16[256,768]{1,0:T(8,128)(2,1)S(1)}, bf16[256,768]{1,0:T(8,128)(2,1)}, u32[]{:S(2)}, u32[]{:S(2)}) collective-permute-start(bf16[256,768]{1,0:T(8,128)(2,1)S(1)} %fusion.65), channel_id=1, source_target_pairs={{0,2},{1,3},{2,0},{3,1},{4,6},{5,7},{6,4},{7,5},{8,10},{9,11},{10,... | collective-permute-start | bytes 1179656 | tf_op jit(solution)/shard_map/ppermute | solution.py:39
  175.9 165.0 %all-gather.24.cloned.1.call-start = ((), (), s32[]{:S(2)}) async-start(), calls=%async_computation.18 | async-start | bytes 1327104 | tf_op jit(solution)/shard_map/all_gather | solution.py:117
  220.3 11.5 %collective-permute-start.6 = (bf16[256,768]{1,0:T(8,128)(2,1)}, bf16[256,768]{1,0:T(8,128)(2,1)}, u32[]{:S(2)}, u32[]{:S(2)}) collective-permute-start(bf16[256,768]{1,0:T(8,128)(2,1)} %fusion.64), channel_id=1, source_target_pairs={{0,2},{1,3},{2,0},{3,1},{4,6},{5,7},{6,4},{7,5},{8,10},{9,11},{10,... | collective-permute-start | bytes 1179656 | tf_op jit(solution)/shard_map/ppermute | solution.py:39
  222.4 133.4 %all-gather.26.cloned.1.call-start = ((), (), s32[]{:S(2)}) async-start(), calls=%async_computation.19 | async-start | bytes 1327104 | tf_op jit(solution)/shard_map/all_gather | solution.py:117
  235.4 65.2 %collective-permute-start.7 = (bf16[256,768]{1,0:T(8,128)(2,1)S(1)}, bf16[256,768]{1,0:T(8,128)(2,1)S(1)}, u32[]{:S(2)}, u32[]{:S(2)}) collective-permute-start(bf16[256,768]{1,0:T(8,128)(2,1)S(1)} %get-tuple-element.83), channel_id=1, source_target_pairs={{0,1},{1,0},{2,3},{3,2},{4,5},{5,4},{6,7},{7,6},{8,9},{9,8},{10,11... | collective-permute-start | bytes 1179656 | tf_op jit(solution)/shard_map/ppermute | solution.py:39
  315.1 11.5 %collective-permute-start.9 = (bf16[256,768]{1,0:T(8,128)(2,1)}, bf16[256,768]{1,0:T(8,128)(2,1)}, u32[]{:S(2)}, u32[]{:S(2)}) collective-permute-start(bf16[256,768]{1,0:T(8,128)(2,1)} %fusion.63), channel_id=1, source_target_pairs={{0,2},{1,3},{2,0},{3,1},{4,6},{5,7},{6,4},{7,5},{8,10},{9,11},{10,... | collective-permute-start | bytes 1179656 | tf_op jit(solution)/shard_map/ppermute | solution.py:39
  316.6 141.3 %reduce-scatter.17.cloned.1.call-start = ((), (), s32[]{:S(2)}) async-start(), calls=%async_computation.12 | async-start | bytes 331776 | tf_op jit(solution)/shard_map/reduce_scatter | solution.py:121
  384.7 124.0 %reduce-scatter.19.cloned.1.call-start = ((), (), s32[]{:S(2)}) async-start(), calls=%async_computation.13 | async-start | bytes 1327104 | tf_op jit(solution)/shard_map/reduce_scatter | solution.py:121
  391.2 184.3 %reduce-scatter.23.cloned.1.call-start = ((), (), s32[]{:S(2)}) async-start(), calls=%async_computation.15 | async-start | bytes 1327104 | tf_op jit(solution)/shard_map/reduce_scatter | solution.py:121
  392.6 11.5 %collective-permute-start.17 = (bf16[256,768]{1,0:T(8,128)(2,1)S(1)}, bf16[256,768]{1,0:T(8,128)(2,1)S(1)}, u32[]{:S(2)}, u32[]{:S(2)}) collective-permute-start(bf16[256,768]{1,0:T(8,128)(2,1)S(1)} %fusion.60), channel_id=1, source_target_pairs={{0,2},{1,3},{2,0},{3,1},{4,6},{5,7},{6,4},{7,5},{8,10},{9,11},{10,... | collective-permute-start | bytes 1179656 | tf_op jit(solution)/shard_map/ppermute | solution.py:39
  408.7 232.4 %reduce-scatter.11.cloned.1.call-start = ((), (), s32[]{:S(2)}) async-start(), calls=%async_computation.9 | async-start | bytes 1105920 | tf_op jit(solution)/shard_map/reduce_scatter | solution.py:121
  415.3 11.3 %collective-permute-start.20 = (bf16[256,768]{1,0:T(8,128)(2,1)S(1)}, bf16[256,768]{1,0:T(8,128)(2,1)}, u32[]{:S(2)}, u32[]{:S(2)}) collective-permute-start(bf16[256,768]{1,0:T(8,128)(2,1)S(1)} %fusion.59), channel_id=1, source_target_pairs={{0,2},{1,3},{2,0},{3,1},{4,6},{5,7},{6,4},{7,5},{8,10},{9,11},{10,... | collective-permute-start | bytes 1179656 | tf_op jit(solution)/shard_map/ppermute | solution.py:39
  418.7 285.7 %reduce-scatter.13.cloned.1.call-start = ((), (), s32[]{:S(2)}) async-start(), calls=%async_computation.10 | async-start | bytes 331776 | tf_op jit(solution)/shard_map/reduce_scatter | solution.py:121
  435.1 334.8 %reduce-scatter.15.cloned.1.call-start = ((), (), s32[]{:S(2)}) async-start(), calls=%async_computation.11 | async-start | bytes 1327104 | tf_op jit(solution)/shard_map/reduce_scatter | solution.py:121
  438.8 398.5 %reduce-scatter.21.cloned.1.call-start = ((), (), s32[]{:S(2)}) async-start(), calls=%async_computation.14 | async-start | bytes 1327104 | tf_op jit(solution)/shard_map/reduce_scatter | solution.py:121
  510.3 90.5 %collective-permute-start.25 = (bf16[120,768]{1,0:T(8,128)(2,1)}, bf16[120,768]{1,0:T(8,128)(2,1)}, u32[]{:S(2)}, u32[]{:S(2)}) collective-permute-start(bf16[120,768]{1,0:T(8,128)(2,1)} %pad_maximum_fusion.15), channel_id=1, source_target_pairs={{0,0},{4,1},{8,2},{12,3},{16,4},{20,5},{24,6},{28,7},{1,8},{5,9},{... | collective-permute-start | bytes 552968 | tf_op jit(solution)/shard_map/ppermute | solution.py:240
  587.2 316.7 %reduce-scatter.9.cloned.1.call-start = ((), (), s32[]{:S(2)}) async-start(), calls=%async_computation.8 | async-start | bytes 1105920 | tf_op jit(solution)/shard_map/reduce_scatter | solution.py:121
  600.4 42.0 %collective-permute-start.22 = (bf16[256,768]{1,0:T(8,128)(2,1)S(1)}, bf16[256,768]{1,0:T(8,128)(2,1)S(1)}, u32[]{:S(2)}, u32[]{:S(2)}) collective-permute-start(bf16[256,768]{1,0:T(8,128)(2,1)S(1)} %bitcast.344), channel_id=1, source_target_pairs={{0,1},{1,0},{2,3},{3,2},{4,5},{5,4},{6,7},{7,6},{8,9},{9,8},{10,11... | collective-permute-start | bytes 1179656 | tf_op jit(solution)/shard_map/ppermute | solution.py:39
  643.2 17.8 %collective-permute-start.23 = (bf16[256,768]{1,0:T(8,128)(2,1)}, bf16[256,768]{1,0:T(8,128)(2,1)}, u32[]{:S(2)}, u32[]{:S(2)}) collective-permute-start(bf16[256,768]{1,0:T(8,128)(2,1)} %fusion.58), channel_id=1, source_target_pairs={{0,2},{1,3},{2,0},{3,1},{4,6},{5,7},{6,4},{7,5},{8,10},{9,11},{10,... | collective-permute-start | bytes 1179656 | tf_op jit(solution)/shard_map/ppermute | solution.py:39
  770.8 77.6 %collective-permute-start.24 = (bf16[120,768]{1,0:T(8,128)(2,1)S(1)}, bf16[120,768]{1,0:T(8,128)(2,1)S(1)}, u32[]{:S(2)}, u32[]{:S(2)}) collective-permute-start(bf16[120,768]{1,0:T(8,128)(2,1)S(1)} %pad_maximum_fusion.14), channel_id=1, source_target_pairs={{0,0},{4,1},{8,2},{12,3},{16,4},{20,5},{24,6},{28,7},{1,8},{5,9},{... | collective-permute-start | bytes 552968 | tf_op jit(solution)/shard_map/ppermute | solution.py:240
  (115 other events, 1012.3 us)
Sparse Core Ops, SparseCore 0:
  13.3 49.8 all-gather.19
  176.0 38.6 all-gather.21
  222.6 48.5 all-gather.23
  316.7 39.0 all-gather.25
  384.8 57.5 reduce-scatter.16
  445.7 62.9 reduce-scatter.18
  512.1 63.3 reduce-scatter.22
  578.8 62.3 reduce-scatter.10
  644.8 57.6 reduce-scatter.12
  706.7 63.1 reduce-scatter.14
  774.2 63.0 reduce-scatter.20
  841.4 62.3 reduce-scatter.8

commit v2 on v1

v2 whole, which is shorter than its diff:
```python
import functools
import jax
import jax.numpy as jnp
from jax import lax
from jax.experimental import pallas as pl
from jax.experimental.pallas import tpu as pltpu
from jax.sharding import PartitionSpec as P

H = 12
EPSILON = 1e-05
FLOOR_VALUE = -1e30
BF = jnp.bfloat16
F32 = jnp.float32
VM = pl.BlockSpec(memory_space=pltpu.VMEM)
SM = pl.BlockSpec(memory_space=pltpu.SMEM)
GELU_A = 0.7978845608028654
GELU_B = 0.044715


def dot(a, b, ca, cb):
    return lax.dot_general(a, b, (((ca,), (cb,)), ((), ())), preferred_element_type=F32)


def call(kernel, outs, ins, scratch=(), flops=0, name=None):
    moved = sum(a.size * a.dtype.itemsize for a in ins)
    return pl.pallas_call(
        kernel,
        out_shape=[jax.ShapeDtypeStruct(s, t) for s, t in outs],
        in_specs=[SM if a.dtype == jnp.int32 and a.ndim == 1 else VM for a in ins],
        out_specs=[VM] * len(outs),
        scratch_shapes=list(scratch),
        compiler_params=pltpu.CompilerParams(vmem_limit_bytes=40 * 1024 * 1024),
        cost_estimate=pl.CostEstimate(flops=flops, bytes_accessed=moved, transcendentals=0),
        name=name,
    )(*ins)


def at(index, rows):
    return pl.ds(pl.multiple_of(index * rows, rows), rows)


class Rows:
    def __init__(self, arrays, plan, size):
        self.arrays, self.plan, self.size = arrays, plan, size
        self.shape = (size * len(plan), arrays[0].shape[1])

    def scratch(self):
        return pltpu.VMEM(self.shape, BF)

    def load(self, refs, scratch, me):
        for index, start, relative, place in self.plan:
            place = me ^ place if relative else place
            target = at(place, self.size) if relative else slice(place * self.size, (place + 1) * self.size)
            scratch[target, :] = refs[index][start : start + self.size, :]


def take_refs(refs, *weights):
    return [[refs.pop(0) for unused in w.arrays] for w in weights]


def norm_parts(values):
    average = jnp.mean(values, axis=-1, keepdims=True)
    centered = values - average
    spread = jnp.mean(centered * centered, axis=-1, keepdims=True)
    inverse = lax.rsqrt(spread + EPSILON)
    return centered * inverse, inverse


def block_allowed(info, kept_ref, b, block, keys):
    i = b * block + lax.broadcasted_iota(jnp.int32, (block, 1), 0)
    j = lax.broadcasted_iota(jnp.int32, (1, keys), 1)

    def segment(t):
        total = jnp.zeros_like(t)
        for n in range(2, info.shape[0]):
            total = total + jnp.where(t >= info[n], 1, 0)
        return total

    same = segment(i) == segment(j)
    itself = i == j
    return same & (j <= i) & ((kept_ref[:, :keys] > 0) | itself)


def gather_halves(low, own, other, full):
    block = own.shape[0] // 2
    for i in range(2):
        full[at(2 * i + low, block), :] = own[i * block : (i + 1) * block, :]
        full[at(2 * i + 1 - low, block), :] = other[i * block : (i + 1) * block, :]


def split_halves(low, full, kept, sent):
    block = kept.shape[0] // 2
    for i in range(2):
        kept[i * block : (i + 1) * block, :] = full[at(2 * i + low, block), :].astype(kept.dtype)
        sent[i * block : (i + 1) * block, :] = full[at(2 * i + 1 - low, block), :].astype(sent.dtype)


def attention_forward_kernel(first, signed, qkv, heads, *refs):
    refs = list(refs)
    info, kept_ref = refs.pop(0), refs.pop(0)
    if first:
        tokens = refs.pop(0)
    else:
        own, other = refs.pop(0), refs.pop(0)
    (pieces,) = take_refs(refs, qkv)
    w_out = refs.pop(0)
    x_ref, proj_ref, att_ref, lse_ref, sent, kept = [refs.pop(0) for unused in range(6)]
    if first:
        stream, vec_ref = refs.pop(0), refs.pop(0)
    w, partial = refs
    me, low = info[0], info[1]
    qkv.load(pieces, w, me)
    part = w_out.shape[0]
    hd = part // heads
    group, width = x_ref.shape
    block = group // 4
    if first:
        tail = w.shape[1] - 3 * part
        pick = lax.broadcasted_iota(jnp.int32, (8, tail), 0) == lax.broadcasted_iota(jnp.int32, (8, tail), 1)
        vec = dot(pick.astype(F32).astype(BF), w[:, 3 * part :], 1, 1)
        vec_ref[...] = vec
        for b in range(4):
            values = tokens[b * block : (b + 1) * block, :].astype(F32)
            normal, unused = norm_parts(values)
            x_ref[b * block : (b + 1) * block, :] = (normal * vec[0:1] + vec[4:5]).astype(BF)
        for i in range(2):
            stream[i * block : (i + 1) * block, :] = tokens[at(2 * i + low, block), :].astype(F32)
    else:
        gather_halves(low, own, other, x_ref)
    proj_ref[...] = dot(x_ref[...], w[...], 1, 0).astype(BF)
    scale = hd ** (-0.5)
    for b in range(4):
        keys = (b + 1) * block
        rows = slice(b * block, keys)
        allowed = block_allowed(info, kept_ref, b, block, keys)
        for h in range(heads):
            q = proj_ref[rows, h * hd : (h + 1) * hd] * scale
            k = proj_ref[:keys, part + h * hd : part + (h + 1) * hd]
            v = proj_ref[:keys, 2 * part + h * hd : 2 * part + (h + 1) * hd]
            scores = dot(q, k, 1, 1)
            magnitude = jnp.abs(scores) if signed else scores
            masked = jnp.where(allowed, magnitude, FLOOR_VALUE)
            peak = jnp.max(masked, axis=-1, keepdims=True)
            raised = jnp.exp(masked - peak)
            total = jnp.sum(raised, axis=-1, keepdims=True)
            if signed:
                lifted = jnp.where(allowed, raised - jnp.exp(-peak), 0.0)
                raised = jnp.where(scores < 0, -lifted, lifted)
            weights = (raised * (1.0 / total)).astype(BF)
            att_ref[rows, h * hd : (h + 1) * hd] = dot(weights, v, 1, 0).astype(BF)
            lse_ref[rows, h : h + 1] = peak + jnp.log(total)
    partial[...] = dot(att_ref[...], w_out[...], 1, 0)
    split_halves(low, partial, kept, sent)


def attention_forward(first, signed, info, kept, x, qkv, w_out, heads):
    width = w_out.shape[1]
    group = kept.shape[1]
    part = w_out.shape[0]
    wide = qkv.shape[1]
    outs = [((group, width), BF), ((group, wide), BF), ((group, part), BF), ((group, 128), F32), ((group // 2, width), BF), ((group // 2, width), F32)]
    if first:
        outs += [((group // 2, width), F32), ((8, width), F32)]
    return call(
        functools.partial(attention_forward_kernel, first, signed, qkv, heads),
        outs,
        [info, kept, *x, *qkv.arrays, w_out],
        [qkv.scratch(), pltpu.VMEM((group, width), F32)],
        flops=2 * group * width * 4 * part,
        name="attend",
    )


def gelu_parts(v):
    inner = GELU_A * (v + GELU_B * v * v * v)
    return jnp.tanh(inner)


def feed_forward_kernel(fc, proj, *refs):
    refs = list(refs)
    info, own, other = [refs.pop(0) for unused in range(3)]
    fc_refs, proj_refs = take_refs(refs, fc, proj)
    hidden, active, sent, kept, w, w_proj = refs
    fc.load(fc_refs, w, info[0])
    proj.load(proj_refs, w_proj, info[0])
    half = own.shape[0]
    ff = w_proj.shape[0]
    step = ff // 3
    for index, (x, target) in enumerate(((other, sent), (own, kept))):
        start = (1 - index) * half
        total = None
        for f in range(3):
            cols = slice(f * step, (f + 1) * step)
            hid = dot(x[...], w[:, cols], 1, 0)
            hidden[start : start + half, cols] = hid
            act = (0.5 * hid * (1.0 + gelu_parts(hid))).astype(BF)
            active[start : start + half, cols] = act
            term = dot(act, w_proj[cols, :], 1, 0)
            total = term if total is None else total + term
        target[...] = total.astype(target.dtype)


def feed_forward(info, own, other, fc, proj):
    half, width = own.shape
    ff = proj.shape[0]
    outs = [((2 * half, ff), F32), ((2 * half, ff), BF), ((half, width), BF), ((half, width), F32)]
    return call(
        functools.partial(feed_forward_kernel, fc, proj),
        outs,
        [info, own, other, *fc.arrays, *proj.arrays],
        [fc.scratch(), proj.scratch()],
        flops=8 * half * width * ff,
        name="feed",
    )


def norm_kernel(row, stream, near, far, vec, middle, normed):
    values = stream[...] + (near[...].astype(F32) + far[...].astype(F32))
    middle[...] = values
    normal, unused = norm_parts(values)
    normed[...] = (normal * vec[row : row + 1, :] + vec[row + 4 : row + 5, :]).astype(BF)


def norm_after(row, stream, near, far, vec):
    shape = stream.shape
    return call(functools.partial(norm_kernel, row), [(shape, F32), (shape, BF)], [stream, near, far, vec], name="norm")


def feed_backward_kernel(fc, proj, *refs):
    refs = list(refs)
    info, own, other, hidden = [refs.pop(0) for unused in range(4)]
    fc_refs, proj_refs = take_refs(refs, fc, proj)
    grad_hidden, sent, kept, w, w_proj = refs
    fc.load(fc_refs, w, info[0])
    proj.load(proj_refs, w_proj, info[0])
    half = own.shape[0]
    ff = w_proj.shape[0]
    step = ff // 3
    for index, (g, target) in enumerate(((other, sent), (own, kept))):
        start = (1 - index) * half
        total = None
        for f in range(3):
            cols = slice(f * step, (f + 1) * step)
            grad_active = dot(g[...], w_proj[cols, :], 1, 1)
            v = hidden[start : start + half, cols]
            t = gelu_parts(v)
            slope = 0.5 * (1.0 + t) + 0.5 * v * (1.0 - t * t) * (GELU_A * (1.0 + 3.0 * GELU_B * v * v))
            gh = (slope * grad_active).astype(BF)
            grad_hidden[start : start + half, cols] = gh
            term = dot(gh, w[:, cols], 1, 1)
            total = term if total is None else total + term
        target[...] = total.astype(target.dtype)


def feed_backward(info, own, other, hidden, fc, proj):
    half, width = own.shape
    ff = proj.shape[0]
    outs = [((2 * half, ff), BF), ((half, width), BF), ((half, width), F32)]
    return call(
        functools.partial(feed_backward_kernel, fc, proj),
        outs,
        [info, own, other, hidden, *fc.arrays, *proj.arrays],
        [fc.scratch(), proj.scratch()],
        flops=8 * half * width * ff,
        name="feed_back",
    )


def norm_backward_kernel(row, grad, near, far, source, vec, out, low, sums):
    incoming = near[...].astype(F32) + far[...].astype(F32)
    normal, inverse = norm_parts(source[...])
    grad_normal = incoming * vec[row : row + 1, :]
    mean_grad = jnp.mean(grad_normal, axis=-1, keepdims=True)
    mean_cross = jnp.mean(grad_normal * normal, axis=-1, keepdims=True)
    value = grad[...].astype(F32) + inverse * (grad_normal - mean_grad - normal * mean_cross)
    out[...] = value
    low[...] = value.astype(BF)
    sums[0:1, :] = jnp.sum(incoming * normal, axis=0, keepdims=True)
    sums[1:2, :] = jnp.sum(incoming, axis=0, keepdims=True)


def norm_back(row, grad, near, far, source, vec):
    shape = source.shape
    return call(
        functools.partial(norm_backward_kernel, row),
        [(shape, F32), (shape, BF), ((2, shape[1]), F32)],
        [grad, near, far, source, vec],
        name="norm_back",
    )


def attention_backward_kernel(signed, qkv, heads, *refs):
    refs = list(refs)
    info, kept_ref, own, other, proj, lse = [refs.pop(0) for unused in range(6)]
    (pieces,) = take_refs(refs, qkv)
    w_out, gm_ref, gp_ref, sent, kept, w, partial, gatt, gk_sum, gv_sum = refs
    me, low = info[0], info[1]
    qkv.load(pieces, w, me)
    part = w_out.shape[0]
    hd = part // heads
    group = gm_ref.shape[0]
    block = group // 4
    gather_halves(low, own, other, gm_ref)
    gatt[...] = dot(gm_ref[...], w_out[...], 1, 1).astype(BF)
    scale = hd ** (-0.5)
    gp_ref[:, 3 * part :] = jnp.zeros((group, gp_ref.shape[1] - 3 * part), BF)
    for b in reversed(range(4)):
        keys = (b + 1) * block
        rows = slice(b * block, keys)
        allowed = block_allowed(info, kept_ref, b, block, keys)
        for h in range(heads):
            cols = slice(h * hd, (h + 1) * hd)
            q = proj[rows, h * hd : (h + 1) * hd] * scale
            k = proj[:keys, part + h * hd : part + (h + 1) * hd]
            v = proj[:keys, 2 * part + h * hd : 2 * part + (h + 1) * hd]
            g = gatt[rows, h * hd : (h + 1) * hd]
            level = lse[rows, h : h + 1]
            scores = dot(q, k, 1, 1)
            magnitude = jnp.abs(scores) if signed else scores
            absolute = jnp.exp(jnp.where(allowed, magnitude, FLOOR_VALUE) - level)
            grad_weights = dot(g, v, 1, 1)
            if signed:
                lifted = jnp.where(allowed, absolute - jnp.exp(-level), 0.0)
                weights = jnp.where(scores < 0, -lifted, lifted)
                delta = jnp.sum(grad_weights * weights, axis=-1, keepdims=True)
                shift = jnp.where(scores > 0, delta, jnp.where(scores < 0, -delta, 0.0))
            else:
                weights = absolute
                shift = jnp.sum(grad_weights * weights, axis=-1, keepdims=True)
            gs = (absolute * (grad_weights - shift)).astype(BF)
            gp_ref[rows, h * hd : (h + 1) * hd] = (dot(gs, k, 1, 0) * scale).astype(BF)
            gk = dot(gs, q, 0, 0)
            gv = dot(weights.astype(BF), g, 0, 0)
            if b == 3:
                gk_sum[h] = gk
                gv_sum[h] = gv
            else:
                gk_sum[h, :keys] += gk
                gv_sum[h, :keys] += gv
    for h in range(heads):
        gp_ref[:, part + h * hd : part + (h + 1) * hd] = gk_sum[h].astype(BF)
        gp_ref[:, 2 * part + h * hd : 2 * part + (h + 1) * hd] = gv_sum[h].astype(BF)
    partial[...] = dot(gp_ref[...], w[...], 1, 1)
    split_halves(low, partial, kept, sent)


def attention_backward(signed, info, kept, own, other, proj, lse, qkv, w_out, heads):
    half, width = own.shape
    group = 2 * half
    part = w_out.shape[0]
    wide = qkv.shape[1]
    outs = [((group, width), BF), ((group, wide), BF), ((half, width), BF), ((half, width), F32)]
    return call(
        functools.partial(attention_backward_kernel, signed, qkv, heads),
        outs,
        [info, kept, own, other, proj, lse, *qkv.arrays, w_out],
        [
            qkv.scratch(),
            pltpu.VMEM((group, width), F32),
            pltpu.VMEM((group, part), BF),
            pltpu.VMEM((heads, group, part // heads), F32),
            pltpu.VMEM((heads, group, part // heads), F32),
        ],
        flops=2 * group * width * 4 * part,
        name="attend_back",
    )


def outer_kernel(parts, sizes, relative, *refs):
    info = refs[0]
    ins, outs, scratch = refs[1 : 1 + 2 * len(sizes)], refs[1 + 2 * len(sizes) : -1], refs[-1]
    start = 0
    for i, slot in enumerate(sizes):
        left, right = ins[2 * i], ins[2 * i + 1]
        rows = left.shape[1]
        size = rows // parts
        scratch[:rows, :] = dot(left[...], right[...], 0, 0)
        if relative:
            sent, kept = outs
            for j in range(parts // 2):
                target = info[0] ^ (2 * j)
                kept[j, start : start + size, :] = scratch[at(target, size), :].astype(BF)
                sent[j, start : start + size, :] = scratch[at(target ^ 1, size), :].astype(BF)
                if slot > size:
                    kept[j, start + size : start + slot, :] = jnp.zeros((slot - size, scratch.shape[1]), BF)
                    sent[j, start + size : start + slot, :] = jnp.zeros((slot - size, scratch.shape[1]), BF)
        else:
            for j in range(parts):
                outs[0][j, start : start + size, :] = scratch[j * size : (j + 1) * size, :].astype(BF)
                if slot > size:
                    outs[0][j, start + size : start + slot, :] = jnp.zeros((slot - size, scratch.shape[1]), BF)
        start += slot


def slot_of(size):
    return (size + 15) // 16 * 16


def outer(parts, info, pairs, relative):
    sizes = [slot_of(left.shape[1] // parts) for left, right in pairs]
    cols = pairs[0][1].shape[1]
    if relative:
        outs = [((parts // 2, sum(sizes), cols), BF)] * 2
    else:
        outs = [((parts, sum(sizes), cols), BF)]
    return call(
        functools.partial(outer_kernel, parts, sizes, relative),
        outs,
        [info] + [a for pair in pairs for a in pair],
        [pltpu.VMEM((max(left.shape[1] for left, right in pairs), cols), F32)],
        flops=sum(2 * left.shape[0] * left.shape[1] * cols for left, right in pairs),
        name="outer",
    )


def swap(x, axis, bit):
    size = lax.axis_size(axis)
    return lax.ppermute(x, axis, [(i, i ^ bit) for i in range(size)])


def row_moves(pb, ka):
    span = pb // ka
    return [(p * ka + k, ((p % span) * ka + k) * ka + p // span) for p in range(pb) for k in range(ka)]


def gather_rows(x):
    return lax.all_gather(x, "pb", axis=0, tiled=True)


def whole_rows(x, parts, start, size):
    piece = x.shape[0] // parts
    return Rows([x], [(0, p * piece + start, False, p) for p in range(parts)], size)


def spread_rows(x, parts):
    if parts > 8:
        return whole_rows(gather_rows(x), parts, 0, x.shape[0])
    near = [x] + [swap(x, "pb", 2 * d) for d in range(1, parts // 2)]
    far = swap(jnp.concatenate(near, axis=0), "pb", 1)
    rows = x.shape[0]
    plan = [(d, 0, True, 2 * d) for d in range(parts // 2)]
    plan += [(parts // 2, d * rows, True, 2 * d + 1) for d in range(parts // 2)]
    return Rows(near + [far], plan, rows)


def sum_rows(info, pairs, parts):
    if parts > 8:
        (x,) = outer(parts, info, pairs, False)
        return lax.psum_scatter(x.reshape(-1, x.shape[2]), "pb", scatter_dimension=0, tiled=True)
    sent, kept = outer(parts, info, pairs, True)
    near = (kept.astype(F32) + swap(sent, "pb", 1).astype(F32)).astype(BF)
    total = near[0].astype(F32)
    for d in range(1, parts // 2):
        total = total + swap(near[d], "pb", 2 * d).astype(F32)
    return total.astype(BF)


def reduce_halves(sent, kept):
    near = (kept + swap(sent, "ka", 1).astype(F32)).astype(BF)
    return near, swap(near, "ka", 2)


def on_device(tokens, cotangent, lengths, keep_mask, w_qkv, w_out, w_fc, w_proj, norm_gain, norm_bias):
    rows, width = tokens.shape
    pb = lax.axis_size("pb")
    ka = lax.axis_size("ka")
    me = lax.axis_index("ka")
    low, high = me % 2, me // 2
    heads = H // ka
    part = width // ka
    ff = w_fc.shape[2]
    ff_part = ff // ka
    d_rows = w_qkv.shape[0]
    out_rows = w_out.shape[0] // ka
    proj_rows = w_proj.shape[0] // ka
    wide = (3 * part + 8 + 127) // 128 * 128
    moves = row_moves(pb, ka)
    bounds = jnp.cumsum(lengths[0])
    info = jnp.concatenate([jnp.stack([lax.axis_index("pb"), low]).astype(jnp.int32), bounds.astype(jnp.int32)])

    local_qkv = lax.dynamic_index_in_dim(w_qkv.reshape(d_rows, 2, 3, ka, part), me, 3, False).reshape(d_rows, 2, 3 * part)
    vectors = jnp.concatenate([norm_gain, norm_bias], axis=1)
    first = jnp.concatenate([local_qkv[:, 0], vectors, jnp.zeros((d_rows, wide - 3 * part - 8), BF)], axis=1)
    second = jnp.concatenate([local_qkv[:, 1], jnp.zeros((d_rows, wide - 3 * part), BF)], axis=1)
    local_fc = lax.dynamic_slice_in_dim(w_fc, me * ff_part, ff_part, 2)
    local_out = lax.dynamic_slice_in_dim(w_out, me * out_rows, out_rows, 0)
    local_proj = lax.dynamic_slice_in_dim(w_proj, me * proj_rows, proj_rows, 0)
    tall = jnp.concatenate([local_proj[:, 0], local_out[:, 0], local_out[:, 1], local_proj[:, 1]], axis=0)
    tall = lax.ppermute(tall, ("pb", "ka"), moves)
    qkv = [spread_rows(first, pb), None]
    early = proj_rows + 2 * out_rows
    tall_a = gather_rows(tall[:early])
    fc = [spread_rows(local_fc[:, 0], pb), None]
    qkv[1] = spread_rows(second, pb)
    tall_b = gather_rows(jnp.concatenate([local_fc[:, 1], tall[early:]], axis=0))
    fc[1] = whole_rows(tall_b, pb, 0, d_rows)
    proj = [whole_rows(tall_a, pb, 0, proj_rows), whole_rows(tall_b, pb, d_rows, proj_rows)]
    parts = tall_a.reshape(pb, early, width)
    out = [parts[:, proj_rows + i * out_rows : proj_rows + (i + 1) * out_rows].reshape(part, width) for i in range(2)]

    kept_all = lax.all_gather(keep_mask, "ka", axis=0, tiled=True).reshape(1, -1)
    tokens_all = lax.all_gather(tokens, "ka", axis=0, tiled=True)
    cotangent_all = lax.all_gather(cotangent, "ka", axis=0, tiled=True)

    saved = []
    x = [tokens_all]
    for l in range(2):
        got = attention_forward(l == 0, l == 0, info, kept_all, x, qkv[l], out[l], heads)
        x_all, projected, attended, lse, sent, kept = got[:6]
        if l == 0:
            stream, vec = got[6:]
        near, far = reduce_halves(sent, kept)
        middle, two_own = norm_after(2 * l + 1, stream, near, far, vec)
        two_other = swap(two_own, "ka", 1)
        hidden, active, sent, kept = feed_forward(info, two_own, two_other, fc[l], proj[l])
        saved.append((stream, x_all, projected, attended, lse, middle, two_own, two_other, hidden, active))
        if l == 0:
            near, far = reduce_halves(sent, kept)
            stream, own = norm_after(2, middle, near, far, vec)
            x = [own, swap(own, "ka", 1)]
    near = (kept + swap(sent, "ka", 1).astype(F32)).astype(BF)

    def block(half, which):
        return lax.dynamic_slice_in_dim(half, which * rows, rows, 0)

    far = swap(block(near, 1 - high), "ka", 2)
    output = (block(middle, high) + (block(near, high).astype(F32) + far.astype(F32))).astype(BF)

    cot = cotangent_all.reshape(2, 2, rows, width)
    branch = [lax.dynamic_index_in_dim(cot, i, 1, False).reshape(2 * rows, width) for i in (low, 1 - low)]
    grad = branch[0]
    sums = [None] * 4
    flows = []
    held = []
    for l in (1, 0):
        stream, x_all, projected, attended, lse, middle, two_own, two_other, hidden, active = saved[l]
        grad_hidden, sent, kept = feed_backward(info, branch[0], branch[1], hidden, fc[l], proj[l])
        two = jnp.concatenate([two_own, two_other], axis=0)
        branch_all = jnp.concatenate(branch, axis=0)
        held = [(two, grad_hidden), (active, branch_all)] + held
        if l:
            flows.append(sum_rows(info, held, pb))
            held = []
        near, far = reduce_halves(sent, kept)
        grad, grad_low, sums[2 * l + 1] = norm_back(2 * l + 1, grad, near, far, middle, vec)
        other = swap(grad_low, "ka", 1)
        middle_all, grad_projected, sent, kept = attention_backward(l == 0, info, kept_all, grad_low, other, projected, lse, qkv[l], out[l], heads)
        held = held + [(attended, middle_all)]
        if l == 0:
            flows.append(sum_rows(info, held, pb))
        flows.append(sum_rows(info, [(x_all, grad_projected)], pb))
        near, far = reduce_halves(sent, kept)
        grad, grad_low, sums[2 * l] = norm_back(2 * l, grad, near, far, stream, vec)
        branch = [grad_low, swap(grad_low, "ka", 1)]
    grad_tokens = block(grad, high)

    def cut(flow, *sizes):
        start, found = 0, []
        for size in sizes:
            found.append(flow[start : start + size])
            start += slot_of(size)
        return found

    fc1, proj1 = cut(flows[0], d_rows, proj_rows)
    (qkv1,) = cut(flows[1], d_rows)
    fc0, proj0, out1, out0 = cut(flows[2], d_rows, proj_rows, out_rows, out_rows)
    (qkv0,) = cut(flows[3], d_rows)
    back = [(b, a) for a, b in moves]
    proj1 = lax.ppermute(proj1, ("pb", "ka"), back)
    tall = lax.ppermute(jnp.concatenate([proj0, out0, out1], axis=0), ("pb", "ka"), back)
    late = lax.all_gather(jnp.concatenate([fc1, proj1], axis=0), "ka", axis=0)
    early = lax.all_gather(jnp.concatenate([fc0, tall], axis=0), "ka", axis=0)
    qkvs = [lax.all_gather(v, "ka", axis=0)[:, :, : 3 * part].reshape(ka, d_rows, 3, part).transpose(1, 2, 0, 3).reshape(d_rows, 3 * width) for v in (qkv0, qkv1)]
    fcs = [v[:, :d_rows].transpose(1, 0, 2).reshape(d_rows, ff) for v in (early, late)]
    projs = [v[:, d_rows : d_rows + proj_rows].reshape(-1, width) for v in (early, late)]
    outs = [early[:, d_rows + proj_rows + i * out_rows : d_rows + proj_rows + (i + 1) * out_rows].reshape(-1, width) for i in range(2)]
    summed = [jnp.stack(v, axis=1).astype(F32) for v in (qkvs, outs, fcs, projs)]
    stacked = jnp.concatenate(sums, axis=0) * 0.5
    stacked = lax.psum(stacked, ("pb", "ka"))
    stacked = lax.dynamic_slice_in_dim(stacked, lax.axis_index("pb") * d_rows, d_rows, 1)
    stacked = stacked.reshape(4, 2, d_rows)
    return (output, grad_tokens, *summed, stacked[:, 0].T, stacked[:, 1].T)


def solution(mesh):
    return jax.shard_map(
        on_device,
        mesh=mesh,
        in_specs=(
            P(("pb", "ka"), None),
            P(("pb", "ka"), None),
            P("pb", None),
            P(("pb", "ka")),
            P("pb", None, None),
            P("pb", None, None),
            P("pb", None, None),
            P("pb", None, None),
            P("pb", None),
            P("pb", None),
        ),
        out_specs=(
            P(("pb", "ka"), None),
            P(("pb", "ka"), None),
            P("pb", None, None),
            P("pb", None, None),
            P("pb", None, None),
            P("pb", None, None),
            P("pb", None),
            P("pb", None),
        ),
        check_vma=False,
    )
```

time: 933 us -> 536 us (0.57)
  blocking collectives: 306 us -> 85 us
  waiting for transfers between devices: 424 us -> 211 us
  matrix products: 67.8 us -> 0 us
  starting transfers between devices: 18.6 us -> 86.3 us
  Pallas kernels: 0 us -> 56.3 us
  other arithmetic: 45.2 us -> 17.4 us
  local copies, waits for them, and re-layouts: 45.5 us -> 55.6 us
    reduce_scatter x8 -> x0, waiting for transfers between devices: 318 us -> none  [scatter_rows(): lax.psum_scatter(x.astype(BF), 'pb', scatter_dimension=0, tiled=True)]
    all_gather x13 -> x3, blocking collectives: 245 us -> 24.8 us  [the longest x2 17 us: on_device(): lax.all_gather(v, 'ka', axis=0)[:, :, :3 * part]]
    ppermute x23 -> x50, waiting for transfers between devices: 77.1 us -> 188 us  [swap(): return lax.ppermute(x, axis, [(i, i ^ bit) for i in range(size)])]
    ppermute x23 -> x50, starting transfers between devices: 12.3 us -> 80.7 us  [swap(): return lax.ppermute(x, axis, [(i, i ^ bit) for i in range(size)])]
    dot_general x34 -> x0, matrix products: 57.8 us -> none  [the longest x24 46.7 us: dot(): lax.dot_general(a, b, (((ca,), (cb,)), ((), ())), preferred_element_type=...]
    pallas_call x0 -> x19, Pallas kernels: none -> 56.3 us  [call(): pl.pallas_call(kernel, out_shape=[jax.ShapeDtypeStruct(s, t) for s, t in...]
    reduce_sum x18 -> x0, other arithmetic: 16 us -> none  [the longest x4 6.02 us: norm_backward(): mean_grad = jnp.mean(grad_normal, axis=-1, keepdims=True)]
    unnamed x211 -> x187, local copies, waits for them, and re-layouts: 21.1 us -> 28.9 us
  transfers between devices with their start and end apart: 38 -> 57, of which waited for: 24 -> 26; matrix products, arithmetic and copies ran while one was open for 14% -> 9% of each run, Pallas kernels for 0% -> 7%
where the time goes in v2:
time: 536 us; the launch traced here: 527 us
  waiting for transfers between devices  211 us (39%)
  starting transfers between devices  86.3 us (16%)
  blocking collectives  85 us (16%)
  Pallas kernels  56.3 us (11%)
  local copies, waits for them, and re-layouts  55.6 us (10%)
  other arithmetic  17.4 us (3%)
  between operations  15.6 us (3%)
    ppermute x50, waiting for transfers between devices, swap(): return lax.ppermute(x, axis, [(i, i ^ bit) for i in range(size)])  188 us
    ppermute x50, starting transfers between devices, swap(): return lax.ppermute(x, axis, [(i, i ^ bit) for i in range(size)])  80.7 us
    pallas_call x19, Pallas kernels, call(): pl.pallas_call(kernel, out_shape=[jax.ShapeDtypeStruct(s, t) for s, t in...  56.3 us
    psum x1, blocking collectives, on_device(): stacked = lax.psum(stacked, ('pb', 'ka'))  39.8 us
    unnamed x187, local copies, waits for them, and re-layouts  28.9 us
    all_gather x2, waiting for transfers between devices, gather_rows(): return lax.all_gather(x, 'pb', axis=0, tiled=True)  23.1 us
    all_gather x2, blocking collectives, on_device(): lax.all_gather(v, 'ka', axis=0)[:, :, :3 * part]  17 us
    all_gather x1, blocking collectives, on_device(): tokens_all = lax.all_gather(tokens, 'ka', axis=0, tiled=True)  11.2 us
  transfers between devices with their start and end apart: 57, of which 26 were waited for; matrix products, arithmetic and copies ran while one was open for 9% of the time, Pallas kernels for 7%

profile of v2, /device:TPU:0, one launch (start us, length us, event | category | flops | bytes accessed | tf_op | source)
XLA Modules:
  0.0 527.4 jit_solution(12572279104014938778)
XLA Ops:
  15.1 28.8 %collective-permute-start = (bf16[96,640]{1,0:T(8,128)(2,1)S(1)}, bf16[96,640]{1,0:T(8,128)(2,1)S(1)}, u32[]{:S(2)}, u32[]{:S(2)}) collective-permute-start(bf16[96,640]{1,0:T(8,128)(2,1)S(1)} %pad_maximum_fusion.12.refs_3_.refs_6_), channel_id=1, source_target_pairs={{0,8},{4,12},{8,0},{12,4},{16,24},{20,28},{24,16},{28,20},{1,9},{5... | collective-permute-start | bytes 368648 | tf_op jit(solution)/shard_map/ppermute | solution.py:418
  46.5 7.7 %all-gather.4 = s32[4,1,128]{2,1,0:T(1,128)S(1)} all-gather(s32[1,1,128]{2,1,0:T(1,128)S(1)} %bitcast.144), channel_id=1, replica_groups=mesh['pb'=8,'ka'=4] {'ka'}, dimensions={0}, use_global_device_ids=true | all-gather | bytes 2560 | tf_op jit(solution)/shard_map/all_gather | solution.py:501
  59.5 11.2 %all_gather.40.refs_2_ = bf16[512,768]{1,0:T(8,128)(2,1)S(1)} all-gather(bf16[128,768]{1,0:T(8,128)(2,1)S(1)} %copy-done.80), channel_id=1, replica_groups=mesh['pb'=8,'ka'=4] {'ka'}, dimensions={0}, use_global_device_ids=true | all-gather | bytes 983040 | tf_op jit(solution)/shard_map/all_gather | solution.py:502
  70.7 23.1 %all-gather.10.cloned.1.call-done.refs_8_.refs_9_ = bf16[1152,768]{1,0:T(8,128)(2,1)} async-done(((bf16[144,768]{1,0:T(8,128)(2,1)}), bf16[1152,768]{1,0:T(8,128)(2,1)}) %all-gather.10.cloned.1.call-update) | async-done | bytes 1769488 | tf_op jit(solution)/shard_map/all_gather | solution.py:427
  95.7 7.3 %attend.2 = (bf16[512,768]{1,0:T(8,128)(2,1)S(1)}, bf16[512,640]{1,0:T(8,128)(2,1)S(1)}, bf16[512,192]{1,0:T(8,128)(2,1)S(1)}, f32[512,128]{1,0:T(8,128)S(1)}, b...) custom-call(s32[5]{0:T(128)S(1)} %pad_add_fusion.refs_0_, ...), custom_call_target="tpu_custom_call" | custom-call | flops 603979776 | bytes 2066452 | tf_op jit(solution)/shard_map/attend/pallas_call | solution.py:26
  125.5 14.4 %collective-permute-done.11.refs_7_.refs_8_ = bf16[384,768]{1,0:T(8,128)(2,1)S(1)} collective-permute-done((bf16[384,768]{1,0:T(8,128)(2,1)S(1)}, bf16[384,768]{1,0:T(8,128)(2,1)S(1)}, u32[]{:S(2)}, u32[]{:S(2)}) %collective-permute-start.11) | collective-permute-done | bytes 589856 | tf_op jit(solution)/shard_map/ppermute | solution.py:418
  155.9 8.2 %collective-permute-done.15.refs_5_.refs_7_ = bf16[96,640]{1,0:T(8,128)(2,1)S(1)} collective-permute-done((bf16[96,640]{1,0:T(8,128)(2,1)S(1)}, bf16[96,640]{1,0:T(8,128)(2,1)S(1)}, u32[]{:S(2)}, u32[]{:S(2)}) %collective-permute-start.15) | collective-permute-done | bytes 122912 | tf_op jit(solution)/shard_map/ppermute | solution.py:418
  176.4 8.1 %collective-permute-done.18.refs_8_.refs_10_ = bf16[384,640]{1,0:T(8,128)(2,1)S(1)} collective-permute-done((bf16[384,640]{1,0:T(8,128)(2,1)S(1)}, bf16[384,640]{1,0:T(8,128)(2,1)S(1)}, u32[]{:S(2)}, u32[]{:S(2)}) %collective-permute-start.18) | collective-permute-done | bytes 491552 | tf_op jit(solution)/shard_map/ppermute | solution.py:418
  184.4 5.9 %attend.3 = (bf16[512,768]{1,0:T(8,128)(2,1)S(1)}, bf16[512,640]{1,0:T(8,128)(2,1)S(1)}, bf16[512,192]{1,0:T(8,128)(2,1)S(1)}, f32[512,128]{1,0:T(8,128)S(1)}, b...) custom-call(s32[5]{0:T(128)S(1)} %pad_add_fusion.refs_0_, s32[1,512]{1,0:T(1,128)S(1)} %bitcast.121, ...), custom_call_target="tpu_custom_call" | custom-call | flops 603979776 | bytes 2066452 | tf_op jit(solution)/shard_map/attend/pallas_call | solution.py:26
  194.4 11.1 %collective-permute-done.20.far = bf16[256,768]{1,0:T(8,128)(2,1)} collective-permute-done((bf16[256,768]{1,0:T(8,128)(2,1)}, bf16[256,768]{1,0:T(8,128)(2,1)}, u32[]{:S(2)}, u32[]{:S(2)}) %collective-permute-start.20) | collective-permute-done | bytes 393248 | tf_op jit(solution)/shard_map/ppermute | solution.py:418
  207.7 9.3 %all_gather.43 = bf16[512,768]{1,0:T(8,128)(2,1)S(1)} all-gather(bf16[128,768]{1,0:T(8,128)(2,1)S(1)} %copy-done.81), channel_id=1, replica_groups=mesh['pb'=8,'ka'=4] {'ka'}, dimensions={0}, use_global_device_ids=true | all-gather | bytes 983040 | tf_op jit(solution)/shard_map/all_gather | solution.py:503
  228.6 11.0 %collective-permute-done.25.far = bf16[256,768]{1,0:T(8,128)(2,1)S(1)} collective-permute-done((bf16[256,768]{1,0:T(8,128)(2,1)S(1)}, bf16[256,768]{1,0:T(8,128)(2,1)S(1)}, u32[]{:S(2)}, u32[]{:S(2)}) %collective-permute-start.25) | collective-permute-done | bytes 393248 | tf_op jit(solution)/shard_map/ppermute | solution.py:418
  242.1 6.6 %attend_back.2 = (bf16[512,768]{1,0:T(8,128)(2,1)S(1)}, bf16[512,640]{1,0:T(8,128)(2,1)S(1)}, bf16[256,768]{1,0:T(8,128)(2,1)S(1)}, f32[256,768]{1,0:T(8,128)S(1)}) custom-call(s32[5]{0:T(128)S(1)} %pad_add_fusion.refs_0_, s32[1,512]{1,0:T(1,128)S(1)} %bitcast.122, bf16[256,768]{1,0:T(8,128)(2,1)S(1)} %get-tuple-element.89.refs_2_, ...), custom_call_target="tpu_custom_call" | custom-call | flops 603979776 | bytes 2983956 | tf_op jit(solution)/shard_map/attend_back/pallas_call | solution.py:26
  251.1 10.8 %collective-permute-done.28.far = bf16[256,768]{1,0:T(8,128)(2,1)S(1)} collective-permute-done((bf16[256,768]{1,0:T(8,128)(2,1)S(1)}, bf16[256,768]{1,0:T(8,128)(2,1)S(1)}, u32[]{:S(2)}, u32[]{:S(2)}) %collective-permute-start.28) | collective-permute-done | bytes 393248 | tf_op jit(solution)/shard_map/ppermute | solution.py:418
  273.6 10.8 %collective-permute-done.31.far = bf16[256,768]{1,0:T(8,128)(2,1)S(1)} collective-permute-done((bf16[256,768]{1,0:T(8,128)(2,1)S(1)}, bf16[256,768]{1,0:T(8,128)(2,1)S(1)}, u32[]{:S(2)}, u32[]{:S(2)}) %collective-permute-start.31) | collective-permute-done | bytes 393248 | tf_op jit(solution)/shard_map/ppermute | solution.py:418
  285.2 9.3 %collective-permute-done.48 = bf16[4,192,768]{2,1,0:T(8,128)(2,1)S(1)} collective-permute-done((bf16[4,192,768]{2,1,0:T(8,128)(2,1)S(1)}, bf16[4,192,768]{2,1,0:T(8,128)(2,1)S(1)}, u32[]{:S(2)}, u32[]{:S(2)}) %collective-permute-start.48) | collective-permute-done | bytes 1179680 | tf_op jit(solution)/shard_map/ppermute | solution.py:418
  301.0 7.0 %attend_back.3 = (bf16[512,768]{1,0:T(8,128)(2,1)S(1)}, bf16[512,640]{1,0:T(8,128)(2,1)S(1)}, bf16[256,768]{1,0:T(8,128)(2,1)S(1)}, f32[256,768]{1,0:T(8,128)S(1)}) custom-call(s32[5]{0:T(128)S(1)} %pad_add_fusion.refs_0_, s32[1,512]{1,0:T(1,128)S(1)} %bitcast.123, bf16[256,768]{1,0:T(8,128)(2,1)S(1)} %get-tuple-element.100.refs_2_, ...), custom_call_target="tpu_custom_call" | custom-call | flops 603979776 | bytes 2983956 | tf_op jit(solution)/shard_map/attend_back/pallas_call | solution.py:26
  318.9 6.5 %collective-permute-done.50 = bf16[192,768]{1,0:T(8,128)(2,1)} collective-permute-done((bf16[192,768]{1,0:T(8,128)(2,1)}, bf16[192,768]{1,0:T(8,128)(2,1)}, u32[]{:S(2)}, u32[]{:S(2)}) %collective-permute-start.50) | collective-permute-done | bytes 294944 | tf_op jit(solution)/shard_map/ppermute | solution.py:418
  331.7 29.4 %collective-permute-done.39 = bf16[4,96,640]{2,1,0:T(8,128)(2,1)} collective-permute-done((bf16[4,96,640]{2,1,0:T(8,128)(2,1)}, bf16[4,96,640]{2,1,0:T(8,128)(2,1)}, u32[]{:S(2)}, u32[]{:S(2)}) %collective-permute-start.39) | collective-permute-done | bytes 491552 | tf_op jit(solution)/shard_map/ppermute | solution.py:418
  377.5 17.8 %collective-permute-done.41 = bf16[96,640]{1,0:T(8,128)(2,1)S(1)} collective-permute-done((bf16[96,640]{1,0:T(8,128)(2,1)S(1)}, bf16[96,640]{1,0:T(8,128)(2,1)S(1)}, u32[]{:S(2)}, u32[]{:S(2)}) %collective-permute-start.41) | collective-permute-done | bytes 122912 | tf_op jit(solution)/shard_map/ppermute | solution.py:418
  395.4 15.1 %collective-permute-done.45 = bf16[256,768]{1,0:T(8,128)(2,1)S(1)} collective-permute-done((bf16[256,768]{1,0:T(8,128)(2,1)S(1)}, bf16[256,768]{1,0:T(8,128)(2,1)S(1)}, u32[]{:S(2)}, u32[]{:S(2)}) %collective-permute-start.45) | collective-permute-done | bytes 393248 | tf_op jit(solution)/shard_map/ppermute | solution.py:418
  416.5 8.7 %all-gather.1 = bf16[384,640]{1,0:T(8,128)(2,1)} all-gather(bf16[96,640]{1,0:T(8,128)(2,1)S(1)} %fusion.8), channel_id=3, replica_groups=mesh['pb'=8,'ka'=4] {'ka'}, dimensions={0}, use_global_device_ids=true | all-gather | bytes 614400 | tf_op jit(solution)/shard_map/all_gather | solution.py:573
  452.7 8.4 %all-gather = bf16[384,640]{1,0:T(8,128)(2,1)S(1)} all-gather(bf16[96,640]{1,0:T(8,128)(2,1)S(1)} %fusion.11), channel_id=2, replica_groups=mesh['pb'=8,'ka'=4] {'ka'}, dimensions={0}, use_global_device_ids=true | all-gather | bytes 614400 | tf_op jit(solution)/shard_map/all_gather | solution.py:573
  467.8 39.8 %psum.7 = f32[8,768]{1,0:T(8,128)S(1)} all-reduce(f32[8,768]{1,0:T(8,128)S(1)} %maximum_multiply_fusion), channel_id=1, replica_groups=mesh['pb'=8,'ka'=4] {'pb','ka'}, use_global_device_ids=true, to_apply=%region_1.2 | all-reduce | flops 6144 | bytes 49152 | tf_op jit(solution)/shard_map/psum | solution.py:579
  (380 shorter events, 195.6 us)
Async XLA Ops:
  7.2 86.6 %all-gather.10.cloned.1.call-start = ((), (), s32[]{:S(2)}) async-start(), calls=%async_computation | async-start | bytes 1990656 | tf_op jit(solution)/shard_map/all_gather | solution.py:427
  11.4 205.7 %all-gather.12.cloned.1.call-start = ((), (), s32[]{:S(2)}) async-start(), calls=%async_computation.1 | async-start | bytes 2654208 | tf_op jit(solution)/shard_map/all_gather | solution.py:427
  15.1 39.3 %collective-permute-start = (bf16[96,640]{1,0:T(8,128)(2,1)S(1)}, bf16[96,640]{1,0:T(8,128)(2,1)S(1)}, u32[]{:S(2)}, u32[]{:S(2)}) collective-permute-start(bf16[96,640]{1,0:T(8,128)(2,1)S(1)} %pad_maximum_fusion.12.refs_3_.refs_6_), channel_id=1, source_target_pairs={{0,8},{4,12},{8,0},{12,4},{16,24},{20,28},{24,16},{28,20},{1,9},{5... | collective-permute-start | bytes 368648 | tf_op jit(solution)/shard_map/ppermute | solution.py:418
  59.4 36.2 %collective-permute-start.3 = (bf16[384,640]{1,0:T(8,128)(2,1)S(1)}, bf16[384,640]{1,0:T(8,128)(2,1)S(1)}, u32[]{:S(2)}, u32[]{:S(2)}) collective-permute-start(bf16[384,640]{1,0:T(8,128)(2,1)S(1)} %pad_maximum_fusion.5), channel_id=1, source_target_pairs={{0,4},{4,0},{8,12},{12,8},{16,20},{20,16},{24,28},{28,24},{1,5},{5... | collective-permute-start | bytes 1474568 | tf_op jit(solution)/shard_map/ppermute | solution.py:418
  114.0 317.9 %all-gather.16.cloned.1.call-start = ((), (), s32[]{:S(2)}) async-start(), calls=%async_computation.3 | async-start | bytes 1474560 | tf_op jit(solution)/shard_map/all_gather | solution.py:571
  124.0 15.8 %collective-permute-start.11 = (bf16[384,768]{1,0:T(8,128)(2,1)S(1)}, bf16[384,768]{1,0:T(8,128)(2,1)S(1)}, u32[]{:S(2)}, u32[]{:S(2)}) collective-permute-start(bf16[384,768]{1,0:T(8,128)(2,1)S(1)} %pad_maximum_fusion.4), channel_id=1, source_target_pairs={{0,4},{4,0},{8,12},{12,8},{16,20},{20,16},{24,28},{28,24},{1,5},{5... | collective-permute-start | bytes 1769480 | tf_op jit(solution)/shard_map/ppermute | solution.py:418
  147.0 27.0 %collective-permute-start.13 = (bf16[256,768]{1,0:T(8,128)(2,1)}, bf16[256,768]{1,0:T(8,128)(2,1)}, u32[]{:S(2)}, u32[]{:S(2)}) collective-permute-start(bf16[256,768]{1,0:T(8,128)(2,1)} %add_convert_fusion.10.near), channel_id=1, source_target_pairs={{0,2},{1,3},{2,0},{3,1},{4,6},{5,7},{6,4},{7,5},{8,10},{9,11},{10,... | collective-permute-start | bytes 1179656 | tf_op jit(solution)/shard_map/ppermute | solution.py:418
  155.1 17.1 %collective-permute-start.17 = (bf16[96,640]{1,0:T(8,128)(2,1)S(1)}, bf16[96,640]{1,0:T(8,128)(2,1)S(1)}, u32[]{:S(2)}, u32[]{:S(2)}) collective-permute-start(bf16[96,640]{1,0:T(8,128)(2,1)S(1)} %concatenate.53.refs_4_.refs_6_), channel_id=1, source_target_pairs={{0,24},{4,28},{8,16},{12,20},{16,8},{20,12},{24,0},{28,4},{1,25},{... | collective-permute-start | bytes 368648 | tf_op jit(solution)/shard_map/ppermute | solution.py:418
  266.0 28.4 %collective-permute-start.48 = (bf16[4,192,768]{2,1,0:T(8,128)(2,1)S(1)}, bf16[4,192,768]{2,1,0:T(8,128)(2,1)S(1)}, u32[]{:S(2)}, u32[]{:S(2)}) collective-permute-start(bf16[4,192,768]{2,1,0:T(8,128)(2,1)S(1)} %get-tuple-element.125), channel_id=1, source_target_pairs={{0,4},{4,0},{8,12},{12,8},{16,20},{20,16},{24,28},{28,24},{1,5},{5... | collective-permute-start | bytes 3538952 | tf_op jit(solution)/shard_map/ppermute | solution.py:418
  295.7 22.9 %collective-permute-start.51 = (bf16[192,768]{1,0:T(8,128)(2,1)}, bf16[192,768]{1,0:T(8,128)(2,1)}, u32[]{:S(2)}, u32[]{:S(2)}) collective-permute-start(bf16[192,768]{1,0:T(8,128)(2,1)} %get-tuple-element.158), channel_id=1, source_target_pairs={{0,24},{4,28},{8,16},{12,20},{16,8},{20,12},{24,0},{28,4},{1,25},{... | collective-permute-start | bytes 884744 | tf_op jit(solution)/shard_map/ppermute | solution.py:418
  297.1 28.3 %collective-permute-start.50 = (bf16[192,768]{1,0:T(8,128)(2,1)}, bf16[192,768]{1,0:T(8,128)(2,1)}, u32[]{:S(2)}, u32[]{:S(2)}) collective-permute-start(bf16[192,768]{1,0:T(8,128)(2,1)} %get-tuple-element.159), channel_id=1, source_target_pairs={{0,16},{4,20},{8,24},{12,28},{16,0},{20,4},{24,8},{28,12},{1,17},{... | collective-permute-start | bytes 884744 | tf_op jit(solution)/shard_map/ppermute | solution.py:418
  300.8 24.7 %collective-permute-start.49 = (bf16[192,768]{1,0:T(8,128)(2,1)S(1)}, bf16[192,768]{1,0:T(8,128)(2,1)}, u32[]{:S(2)}, u32[]{:S(2)}) collective-permute-start(bf16[192,768]{1,0:T(8,128)(2,1)S(1)} %get-tuple-element.157), channel_id=1, source_target_pairs={{0,8},{4,12},{8,0},{12,4},{16,24},{20,28},{24,16},{28,20},{1,9},{5... | collective-permute-start | bytes 884744 | tf_op jit(solution)/shard_map/ppermute | solution.py:418
  312.4 54.5 %collective-permute-start.43 = (bf16[4,256,768]{2,1,0:T(8,128)(2,1)}, bf16[4,256,768]{2,1,0:T(8,128)(2,1)}, u32[]{:S(2)}, u32[]{:S(2)}) collective-permute-start(bf16[4,256,768]{2,1,0:T(8,128)(2,1)} %get-tuple-element.121), channel_id=1, source_target_pairs={{0,4},{4,0},{8,12},{12,8},{16,20},{20,16},{24,28},{28,24},{1,5},{5... | collective-permute-start | bytes 4718600 | tf_op jit(solution)/shard_map/ppermute | solution.py:418
  318.6 42.5 %collective-permute-start.39 = (bf16[4,96,640]{2,1,0:T(8,128)(2,1)}, bf16[4,96,640]{2,1,0:T(8,128)(2,1)}, u32[]{:S(2)}, u32[]{:S(2)}) collective-permute-start(bf16[4,96,640]{2,1,0:T(8,128)(2,1)} %get-tuple-element.113), channel_id=1, source_target_pairs={{0,4},{4,0},{8,12},{12,8},{16,20},{20,16},{24,28},{28,24},{1,5},{5... | collective-permute-start | bytes 1474568 | tf_op jit(solution)/shard_map/ppermute | solution.py:418
  328.4 41.5 %collective-permute-start.23 = (bf16[128,768]{1,0:T(8,128)(2,1)}, bf16[128,768]{1,0:T(8,128)(2,1)S(1)}, u32[]{:S(2)}, u32[]{:S(2)}) collective-permute-start(bf16[128,768]{1,0:T(8,128)(2,1)} %constant_dynamic-slice_fusion.6), channel_id=1, source_target_pairs={{0,2},{1,3},{2,0},{3,1},{4,6},{5,7},{6,4},{7,5},{8,10},{9,11},{10,... | collective-permute-start | bytes 589832 | tf_op jit(solution)/shard_map/ppermute | solution.py:418
  331.4 177.6 %all-gather.14.cloned.1.call-start = ((), (), s32[]{:S(2)}) async-start(), calls=%async_computation.2 | async-start | bytes 1843200 | tf_op jit(solution)/shard_map/all_gather | solution.py:572
  362.5 32.7 %collective-permute-start.41 = (bf16[96,640]{1,0:T(8,128)(2,1)S(1)}, bf16[96,640]{1,0:T(8,128)(2,1)S(1)}, u32[]{:S(2)}, u32[]{:S(2)}) collective-permute-start(bf16[96,640]{1,0:T(8,128)(2,1)S(1)} %get-tuple-element.171), channel_id=1, source_target_pairs={{0,16},{4,20},{8,24},{12,28},{16,0},{20,4},{24,8},{28,12},{1,17},{... | collective-permute-start | bytes 368648 | tf_op jit(solution)/shard_map/ppermute | solution.py:418
  366.5 28.8 %collective-permute-start.40 = (bf16[96,640]{1,0:T(8,128)(2,1)S(1)}, bf16[96,640]{1,0:T(8,128)(2,1)S(1)}, u32[]{:S(2)}, u32[]{:S(2)}) collective-permute-start(bf16[96,640]{1,0:T(8,128)(2,1)S(1)} %get-tuple-element.169), channel_id=1, source_target_pairs={{0,8},{4,12},{8,0},{12,4},{16,24},{20,28},{24,16},{28,20},{1,9},{5... | collective-permute-start | bytes 368648 | tf_op jit(solution)/shard_map/ppermute | solution.py:418
  368.9 26.5 %collective-permute-start.46 = (bf16[256,768]{1,0:T(8,128)(2,1)S(1)}, bf16[256,768]{1,0:T(8,128)(2,1)S(1)}, u32[]{:S(2)}, u32[]{:S(2)}) collective-permute-start(bf16[256,768]{1,0:T(8,128)(2,1)S(1)} %get-tuple-element.149), channel_id=1, source_target_pairs={{0,24},{4,28},{8,16},{12,20},{16,8},{20,12},{24,0},{28,4},{1,25},{... | collective-permute-start | bytes 1179656 | tf_op jit(solution)/shard_map/ppermute | solution.py:418
  370.0 40.6 %collective-permute-start.45 = (bf16[256,768]{1,0:T(8,128)(2,1)S(1)}, bf16[256,768]{1,0:T(8,128)(2,1)S(1)}, u32[]{:S(2)}, u32[]{:S(2)}) collective-permute-start(bf16[256,768]{1,0:T(8,128)(2,1)S(1)} %get-tuple-element.150), channel_id=1, source_target_pairs={{0,16},{4,20},{8,24},{12,28},{16,0},{20,4},{24,8},{28,12},{1,17},{... | collective-permute-start | bytes 1179656 | tf_op jit(solution)/shard_map/ppermute | solution.py:418
  372.0 38.5 %collective-permute-start.44 = (bf16[256,768]{1,0:T(8,128)(2,1)S(1)}, bf16[256,768]{1,0:T(8,128)(2,1)S(1)}, u32[]{:S(2)}, u32[]{:S(2)}) collective-permute-start(bf16[256,768]{1,0:T(8,128)(2,1)S(1)} %get-tuple-element.148), channel_id=1, source_target_pairs={{0,8},{4,12},{8,0},{12,4},{16,24},{20,28},{24,16},{28,20},{1,9},{5... | collective-permute-start | bytes 1179656 | tf_op jit(solution)/shard_map/ppermute | solution.py:418
  411.5 18.6 %collective-permute-start.47 = (bf16[144,768]{1,0:T(8,128)(2,1)}, bf16[144,768]{1,0:T(8,128)(2,1)}, u32[]{:S(2)}, u32[]{:S(2)}) collective-permute-start(bf16[144,768]{1,0:T(8,128)(2,1)} %pad_maximum_fusion.11), channel_id=1, source_target_pairs={{0,0},{4,1},{8,2},{12,3},{16,4},{20,5},{24,6},{28,7},{1,8},{5,9},{... | collective-permute-start | bytes 663560 | tf_op jit(solution)/shard_map/ppermute | solution.py:570
  416.4 21.2 %collective-permute-start.35 = (bf16[4,96,640]{2,1,0:T(8,128)(2,1)S(1)}, bf16[4,96,640]{2,1,0:T(8,128)(2,1)}, u32[]{:S(2)}, u32[]{:S(2)}) collective-permute-start(bf16[4,96,640]{2,1,0:T(8,128)(2,1)S(1)} %get-tuple-element.109), channel_id=1, source_target_pairs={{0,4},{4,0},{8,12},{12,8},{16,20},{20,16},{24,28},{28,24},{1,5},{5... | collective-permute-start | bytes 1474568 | tf_op jit(solution)/shard_map/ppermute | solution.py:418
  443.4 23.0 %collective-permute-start.34 = (bf16[256,768]{1,0:T(8,128)(2,1)S(1)}, bf16[256,768]{1,0:T(8,128)(2,1)S(1)}, u32[]{:S(2)}, u32[]{:S(2)}) collective-permute-start(bf16[256,768]{1,0:T(8,128)(2,1)S(1)} %add_convert_fusion.4.near), channel_id=1, source_target_pairs={{0,2},{1,3},{2,0},{3,1},{4,6},{5,7},{6,4},{7,5},{8,10},{9,11},{10,... | collective-permute-start | bytes 1179656 | tf_op jit(solution)/shard_map/ppermute | solution.py:418
  (121 other events, 1316.7 us)
Sparse Core Ops, SparseCore 0:
  11.5 82.2 all-gather.9
  114.1 61.6 all-gather.11
  331.6 48.6 all-gather.15
  432.0 19.8 all-gather.13

commit v3 on v2

--- a/solution.py
+++ b/solution.py
@@ -40,18 +40,24 @@
 
 
 class Rows:
-    def __init__(self, arrays, plan, size):
-        self.arrays, self.plan, self.size = arrays, plan, size
+    def __init__(self, arrays, plan, size, span=0):
+        self.arrays, self.plan, self.size, self.span = arrays, plan, size, span
         self.shape = (size * len(plan), arrays[0].shape[1])
 
     def scratch(self):
-        return pltpu.VMEM(self.shape, BF)
+        return pltpu.VMEM(self.shape, F32 if self.size % 16 else BF)
 
     def load(self, refs, scratch, me):
-        for index, start, relative, place in self.plan:
-            place = me ^ place if relative else place
+        for index, start, p, relative in self.plan:
+            place = me ^ p if relative else p
+            if self.span:
+                place = place_of(place, self.span, len(self.plan) // self.span)
             target = at(place, self.size) if relative else slice(place * self.size, (place + 1) * self.size)
-            scratch[target, :] = refs[index][start : start + self.size, :]
+            scratch[target, :] = refs[index][start : start + self.size, :].astype(scratch.dtype)
+
+
+def place_of(p, span, ka):
+    return (p % span) * ka + p // span if isinstance(p, int) else lax.rem(p, span) * ka + lax.div(p, span)
 
 
 def take_refs(refs, *weights):
@@ -95,21 +101,21 @@
         sent[i * block : (i + 1) * block, :] = full[at(2 * i + 1 - low, block), :].astype(sent.dtype)
 
 
-def attention_forward_kernel(first, signed, qkv, heads, *refs):
+def attention_forward_kernel(first, signed, qkv, out, heads, *refs):
     refs = list(refs)
     info, kept_ref = refs.pop(0), refs.pop(0)
     if first:
         tokens = refs.pop(0)
     else:
         own, other = refs.pop(0), refs.pop(0)
-    (pieces,) = take_refs(refs, qkv)
-    w_out = refs.pop(0)
+    pieces, out_pieces = take_refs(refs, qkv, out)
     x_ref, proj_ref, att_ref, lse_ref, sent, kept = [refs.pop(0) for unused in range(6)]
     if first:
         stream, vec_ref = refs.pop(0), refs.pop(0)
-    w, partial = refs
+    w, w_out, partial = refs
     me, low = info[0], info[1]
     qkv.load(pieces, w, me)
+    out.load(out_pieces, w_out, me)
     part = w_out.shape[0]
     hd = part // heads
     group, width = x_ref.shape
@@ -149,23 +155,22 @@
             weights = (raised * (1.0 / total)).astype(BF)
             att_ref[rows, h * hd : (h + 1) * hd] = dot(weights, v, 1, 0).astype(BF)
             lse_ref[rows, h : h + 1] = peak + jnp.log(total)
-    partial[...] = dot(att_ref[...], w_out[...], 1, 0)
+    partial[...] = dot(att_ref[...], w_out[...].astype(BF), 1, 0)
     split_halves(low, partial, kept, sent)
 
 
-def attention_forward(first, signed, info, kept, x, qkv, w_out, heads):
-    width = w_out.shape[1]
+def attention_forward(first, signed, info, kept, x, qkv, out, heads):
+    part, width = out.shape
     group = kept.shape[1]
-    part = w_out.shape[0]
     wide = qkv.shape[1]
     outs = [((group, width), BF), ((group, wide), BF), ((group, part), BF), ((group, 128), F32), ((group // 2, width), BF), ((group // 2, width), F32)]
     if first:
         outs += [((group // 2, width), F32), ((8, width), F32)]
     return call(
-        functools.partial(attention_forward_kernel, first, signed, qkv, heads),
+        functools.partial(attention_forward_kernel, first, signed, qkv, out, heads),
         outs,
-        [info, kept, *x, *qkv.arrays, w_out],
-        [qkv.scratch(), pltpu.VMEM((group, width), F32)],
+        [info, kept, *x, *qkv.arrays, *out.arrays],
+        [qkv.scratch(), out.scratch(), pltpu.VMEM((group, width), F32)],
         flops=2 * group * width * 4 * part,
         name="attend",
     )
@@ -266,7 +271,7 @@
     )
 
 
-def norm_backward_kernel(row, grad, near, far, source, vec, out, low, sums):
+def norm_backward_kernel(row, grad, near, far, source, vec, out, *rest):
     incoming = near[...].astype(F32) + far[...].astype(F32)
     normal, inverse = norm_parts(source[...])
     grad_normal = incoming * vec[row : row + 1, :]
@@ -274,34 +279,43 @@
     mean_cross = jnp.mean(grad_normal * normal, axis=-1, keepdims=True)
     value = grad[...].astype(F32) + inverse * (grad_normal - mean_grad - normal * mean_cross)
     out[...] = value
+    if not rest:
+        return
+    low, sums = rest
     low[...] = value.astype(BF)
     sums[0:1, :] = jnp.sum(incoming * normal, axis=0, keepdims=True)
     sums[1:2, :] = jnp.sum(incoming, axis=0, keepdims=True)
 
 
-def norm_back(row, grad, near, far, source, vec):
+def norm_back(row, grad, near, far, source, vec, last=False):
     shape = source.shape
     return call(
         functools.partial(norm_backward_kernel, row),
-        [(shape, F32), (shape, BF), ((2, shape[1]), F32)],
+        [(shape, F32)] if last else [(shape, F32), (shape, BF), ((2, shape[1]), F32)],
         [grad, near, far, source, vec],
         name="norm_back",
     )
 
 
-def attention_backward_kernel(signed, qkv, heads, *refs):
+def attention_backward_kernel(first, signed, qkv, out, heads, *refs):
     refs = list(refs)
     info, kept_ref, own, other, proj, lse = [refs.pop(0) for unused in range(6)]
-    (pieces,) = take_refs(refs, qkv)
-    w_out, gm_ref, gp_ref, sent, kept, w, partial, gatt, gk_sum, gv_sum = refs
+    pieces, out_pieces = take_refs(refs, qkv, out)
+    if first:
+        tokens = refs.pop(0)
+    gm_ref, gp_ref, sent, kept = [refs.pop(0) for unused in range(4)]
+    if first:
+        sums = refs.pop(0)
+    w, w_out, partial, gatt, gk_sum, gv_sum = refs
     me, low = info[0], info[1]
     qkv.load(pieces, w, me)
+    out.load(out_pieces, w_out, me)
     part = w_out.shape[0]
     hd = part // heads
     group = gm_ref.shape[0]
     block = group // 4
     gather_halves(low, own, other, gm_ref)
-    gatt[...] = dot(gm_ref[...], w_out[...], 1, 1).astype(BF)
+    gatt[...] = dot(gm_ref[...], w_out[...].astype(BF), 1, 1).astype(BF)
     scale = hd ** (-0.5)
     gp_ref[:, 3 * part :] = jnp.zeros((group, gp_ref.shape[1] - 3 * part), BF)
     for b in reversed(range(4)):
@@ -342,20 +356,33 @@
         gp_ref[:, 2 * part + h * hd : 2 * part + (h + 1) * hd] = gv_sum[h].astype(BF)
     partial[...] = dot(gp_ref[...], w[...], 1, 1)
     split_halves(low, partial, kept, sent)
-
-
-def attention_backward(signed, info, kept, own, other, proj, lse, qkv, w_out, heads):
+    if first:
+        gain = bias = 0.0
+        for b in range(4):
+            rows = slice(b * block, (b + 1) * block)
+            normal, unused = norm_parts(tokens[rows, :].astype(F32))
+            value = partial[rows, :]
+            gain = gain + jnp.sum(value * normal, axis=0, keepdims=True)
+            bias = bias + jnp.sum(value, axis=0, keepdims=True)
+        sums[0:1, :] = gain
+        sums[1:2, :] = bias
+
+
+def attention_backward(first, signed, info, kept, own, other, proj, lse, qkv, out, tokens, heads):
     half, width = own.shape
     group = 2 * half
-    part = w_out.shape[0]
+    part = out.shape[0]
     wide = qkv.shape[1]
     outs = [((group, width), BF), ((group, wide), BF), ((half, width), BF), ((half, width), F32)]
+    if first:
+        outs += [((2, width), F32)]
     return call(
-        functools.partial(attention_backward_kernel, signed, qkv, heads),
+        functools.partial(attention_backward_kernel, first, signed, qkv, out, heads),
         outs,
-        [info, kept, own, other, proj, lse, *qkv.arrays, w_out],
+        [info, kept, own, other, proj, lse, *qkv.arrays, *out.arrays] + ([tokens] if first else []),
         [
             qkv.scratch(),
+            out.scratch(),
             pltpu.VMEM((group, width), F32),
             pltpu.VMEM((group, part), BF),
             pltpu.VMEM((heads, group, part // heads), F32),
@@ -366,29 +393,30 @@
     )
 
 
-def outer_kernel(parts, sizes, relative, *refs):
-    info = refs[0]
-    ins, outs, scratch = refs[1 : 1 + 2 * len(sizes)], refs[1 + 2 * len(sizes) : -1], refs[-1]
+def outer_kernel(parts, plans, relative, *refs):
+    info, scratch = refs[0], refs[-1]
+    outs = refs[-3:-1] if relative else refs[-2:-1]
     start = 0
-    for i, slot in enumerate(sizes):
-        left, right = ins[2 * i], ins[2 * i + 1]
-        rows = left.shape[1]
+    for segments, rows, slot, span in plans:
         size = rows // parts
-        scratch[:rows, :] = dot(left[...], right[...], 0, 0)
-        if relative:
-            sent, kept = outs
-            for j in range(parts // 2):
-                target = info[0] ^ (2 * j)
-                kept[j, start : start + size, :] = scratch[at(target, size), :].astype(BF)
-                sent[j, start : start + size, :] = scratch[at(target ^ 1, size), :].astype(BF)
+
+        def place(p):
+            return place_of(p, span, parts // span) if span else p
+
+        total = None
+        for left, first, right, second, count in segments:
+            term = dot(refs[left][first : first + count, :], refs[right][second : second + count, :], 0, 0)
+            total = term if total is None else total + term
+        scratch[:rows, :] = total
+        for j in range(parts // 2 if relative else parts):
+            if relative:
+                targets = [at(place(info[0] ^ (2 * j + 1)), size), at(place(info[0] ^ (2 * j)), size)]
+            else:
+                targets = [slice(place(j) * size, (place(j) + 1) * size)]
+            for ref, target in zip(outs, targets):
+                ref[j, start : start + size, :] = scratch[target, :].astype(BF)
                 if slot > size:
-                    kept[j, start + size : start + slot, :] = jnp.zeros((slot - size, scratch.shape[1]), BF)
-                    sent[j, start + size : start + slot, :] = jnp.zeros((slot - size, scratch.shape[1]), BF)
-        else:
-            for j in range(parts):
-                outs[0][j, start : start + size, :] = scratch[j * size : (j + 1) * size, :].astype(BF)
-                if slot > size:
-                    outs[0][j, start + size : start + slot, :] = jnp.zeros((slot - size, scratch.shape[1]), BF)
+                    ref[j, start + size : start + slot, :] = jnp.zeros((slot - size, scratch.shape[1]), BF)
         start += slot
 
 
@@ -397,20 +425,34 @@
 
 
 def outer(parts, info, pairs, relative):
-    sizes = [slot_of(left.shape[1] // parts) for left, right in pairs]
-    cols = pairs[0][1].shape[1]
-    if relative:
-        outs = [((parts // 2, sum(sizes), cols), BF)] * 2
-    else:
-        outs = [((parts, sum(sizes), cols), BF)]
+    arrays, plans = [info], []
+
+    def number(a):
+        for n, other in enumerate(arrays):
+            if other is a:
+                return n
+        arrays.append(a)
+        return len(arrays) - 1
+
+    for segments, span in pairs:
+        rows = segments[0][0].shape[1]
+        numbers = [(number(a), first, number(b), second, count) for a, first, b, second, count in segments]
+        plans.append((numbers, rows, slot_of(rows // parts), span))
+    cols = pairs[0][0][0][2].shape[1]
+    tall = sum(p[2] for p in plans)
+    outs = [((parts // 2, tall, cols), BF)] * 2 if relative else [((parts, tall, cols), BF)]
     return call(
-        functools.partial(outer_kernel, parts, sizes, relative),
+        functools.partial(outer_kernel, parts, plans, relative),
         outs,
-        [info] + [a for pair in pairs for a in pair],
-        [pltpu.VMEM((max(left.shape[1] for left, right in pairs), cols), F32)],
-        flops=sum(2 * left.shape[0] * left.shape[1] * cols for left, right in pairs),
+        arrays,
+        [pltpu.VMEM((max(p[1] for p in plans), cols), F32)],
+        flops=sum(2 * p[1] * cols * sum(seg[4] for seg in p[0]) for p in plans),
         name="outer",
     )
+
+
+def tie(*values):
+    return lax.optimization_barrier(values)
 
 
 def swap(x, axis, bit):
@@ -420,50 +462,95 @@
 
 def row_moves(pb, ka):
     span = pb // ka
-    return [(p * ka + k, ((p % span) * ka + k) * ka + p // span) for p in range(pb) for k in range(ka)]
+    return [(p * ka + k, (k * span + p % span) * ka + p // span) for p in range(pb) for k in range(ka)]
 
 
 def gather_rows(x):
     return lax.all_gather(x, "pb", axis=0, tiled=True)
 
 
-def whole_rows(x, parts, start, size):
+def whole_rows(x, parts, start, size, span=0):
     piece = x.shape[0] // parts
-    return Rows([x], [(0, p * piece + start, False, p) for p in range(parts)], size)
-
-
-def spread_rows(x, parts):
+    return Rows([x], [(0, p * piece + start, p, False) for p in range(parts)], size, span)
+
+
+class Spread:
+    def __init__(self, x, parts):
+        self.x, self.parts = x, parts
+        if parts > 8:
+            self.all = gather_rows(x)
+        else:
+            self.near = [x] + [swap(x, "pb", 2 * d) for d in range(1, parts // 2)]
+
+    def turn(self, after):
+        if self.parts > 8:
+            return
+        after, *self.near = tie(after, *self.near)
+        self.far = swap(jnp.concatenate(self.near, axis=0), "pb", 1)
+
+    def rows(self, size=None, span=0):
+        rows, parts = self.x.shape[0], self.parts
+        size = size or rows
+        if parts > 8:
+            return whole_rows(self.all, parts, 0, size, span)
+        plan = [(d, 0, 2 * d, True) for d in range(parts // 2)]
+        plan += [(parts // 2, d * rows, 2 * d + 1, True) for d in range(parts // 2)]
+        return Rows(self.near + [self.far], plan, size, span)
+
+
+def direct_rows(x, parts):
     if parts > 8:
         return whole_rows(gather_rows(x), parts, 0, x.shape[0])
-    near = [x] + [swap(x, "pb", 2 * d) for d in range(1, parts // 2)]
-    far = swap(jnp.concatenate(near, axis=0), "pb", 1)
-    rows = x.shape[0]
-    plan = [(d, 0, True, 2 * d) for d in range(parts // 2)]
-    plan += [(parts // 2, d * rows, True, 2 * d + 1) for d in range(parts // 2)]
-    return Rows(near + [far], plan, rows)
-
-
-def sum_rows(info, pairs, parts):
-    if parts > 8:
-        (x,) = outer(parts, info, pairs, False)
-        return lax.psum_scatter(x.reshape(-1, x.shape[2]), "pb", scatter_dimension=0, tiled=True)
-    sent, kept = outer(parts, info, pairs, True)
-    near = (kept.astype(F32) + swap(sent, "pb", 1).astype(F32)).astype(BF)
-    total = near[0].astype(F32)
-    for d in range(1, parts // 2):
-        total = total + swap(near[d], "pb", 2 * d).astype(F32)
-    return total.astype(BF)
-
-
-def reduce_halves(sent, kept):
-    near = (kept + swap(sent, "ka", 1).astype(F32)).astype(BF)
-    return near, swap(near, "ka", 2)
+    return Rows([x] + [swap(x, "pb", d) for d in range(1, parts)], [(d, 0, d, True) for d in range(parts)], x.shape[0])
+
+
+class Flow:
+    def __init__(self, info, pairs, parts):
+        self.parts = parts
+        if parts > 8:
+            (x,) = outer(parts, info, pairs, False)
+            self.done = lax.psum_scatter(x.reshape(-1, x.shape[2]), "pb", scatter_dimension=0, tiled=True)
+            self.made = self.kept = x
+            return
+        sent, self.kept = outer(parts, info, pairs, True)
+        self.got = swap(sent, "pb", 1)
+        self.made = self.kept
+
+    def turn(self, after):
+        if self.parts > 8:
+            return
+        after, self.kept, self.got = tie(after, self.kept, self.got)
+        near = (self.kept.astype(F32) + self.got.astype(F32)).astype(BF)
+        self.kept = near[0]
+        self.got = [swap(near[d], "pb", 2 * d) for d in range(1, self.parts // 2)]
+
+    def end(self, after):
+        if self.parts > 8:
+            return self.done
+        after, self.kept, *self.got = tie(after, self.kept, *self.got)
+        total = self.kept.astype(F32)
+        for part in self.got:
+            total = total + part.astype(F32)
+        return total.astype(BF)
+
+
+def gather_ka(x):
+    far = swap(x, "ka", 2)
+    both = swap(jnp.stack([x, far]), "ka", 1)
+    me = lax.axis_index("ka")
+    pair = jnp.stack([x, far])
+    even = jnp.where(me % 2 == 0, pair, both)
+    odd = jnp.where(me % 2 == 0, both, pair)
+    first = jnp.where(me < 2, even, even[::-1])
+    second = jnp.where(me < 2, odd, odd[::-1])
+    return [first[0], second[0], first[1], second[1]]
 
 
 def on_device(tokens, cotangent, lengths, keep_mask, w_qkv, w_out, w_fc, w_proj, norm_gain, norm_bias):
     rows, width = tokens.shape
     pb = lax.axis_size("pb")
     ka = lax.axis_size("ka")
+    span = pb // ka
     me = lax.axis_index("ka")
     low, high = me % 2, me // 2
     heads = H // ka
@@ -478,108 +565,154 @@
     bounds = jnp.cumsum(lengths[0])
     info = jnp.concatenate([jnp.stack([lax.axis_index("pb"), low]).astype(jnp.int32), bounds.astype(jnp.int32)])
 
-    local_qkv = lax.dynamic_index_in_dim(w_qkv.reshape(d_rows, 2, 3, ka, part), me, 3, False).reshape(d_rows, 2, 3 * part)
+    def local_qkv(l):
+        return lax.dynamic_index_in_dim(w_qkv[:, l].reshape(d_rows, 3, ka, part), me, 2, False).reshape(d_rows, 3 * part)
+
     vectors = jnp.concatenate([norm_gain, norm_bias], axis=1)
-    first = jnp.concatenate([local_qkv[:, 0], vectors, jnp.zeros((d_rows, wide - 3 * part - 8), BF)], axis=1)
-    second = jnp.concatenate([local_qkv[:, 1], jnp.zeros((d_rows, wide - 3 * part), BF)], axis=1)
-    local_fc = lax.dynamic_slice_in_dim(w_fc, me * ff_part, ff_part, 2)
-    local_out = lax.dynamic_slice_in_dim(w_out, me * out_rows, out_rows, 0)
-    local_proj = lax.dynamic_slice_in_dim(w_proj, me * proj_rows, proj_rows, 0)
-    tall = jnp.concatenate([local_proj[:, 0], local_out[:, 0], local_out[:, 1], local_proj[:, 1]], axis=0)
+    first = jnp.concatenate([local_qkv(0), vectors, jnp.zeros((d_rows, wide - 3 * part - 8), BF)], axis=1)
+    qkv = [direct_rows(first, pb), None]
+    first, w_out_in, w_proj_in = tie(first, w_out, w_proj)
+    local_out = lax.dynamic_slice_in_dim(w_out_in, me * out_rows, out_rows, 0)
+    local_proj = lax.dynamic_slice_in_dim(w_proj_in, me * proj_rows, proj_rows, 0)
+    slot = slot_of(out_rows)
+
+    def filled(x):
+        return jnp.pad(x, ((0, slot - out_rows), (0, 0)))
+
+    tall = jnp.concatenate([filled(local_out[:, 0]), filled(local_out[:, 1]), local_proj[:, 0], local_proj[:, 1]], axis=0)
     tall = lax.ppermute(tall, ("pb", "ka"), moves)
-    qkv = [spread_rows(first, pb), None]
-    early = proj_rows + 2 * out_rows
-    tall_a = gather_rows(tall[:early])
-    fc = [spread_rows(local_fc[:, 0], pb), None]
-    qkv[1] = spread_rows(second, pb)
-    tall_b = gather_rows(jnp.concatenate([local_fc[:, 1], tall[early:]], axis=0))
-    fc[1] = whole_rows(tall_b, pb, 0, d_rows)
-    proj = [whole_rows(tall_a, pb, 0, proj_rows), whole_rows(tall_b, pb, d_rows, proj_rows)]
-    parts = tall_a.reshape(pb, early, width)
-    out = [parts[:, proj_rows + i * out_rows : proj_rows + (i + 1) * out_rows].reshape(part, width) for i in range(2)]
-
     kept_all = lax.all_gather(keep_mask, "ka", axis=0, tiled=True).reshape(1, -1)
     tokens_all = lax.all_gather(tokens, "ka", axis=0, tiled=True)
-    cotangent_all = lax.all_gather(cotangent, "ka", axis=0, tiled=True)
-
-    saved = []
-    x = [tokens_all]
-    for l in range(2):
-        got = attention_forward(l == 0, l == 0, info, kept_all, x, qkv[l], out[l], heads)
-        x_all, projected, attended, lse, sent, kept = got[:6]
-        if l == 0:
-            stream, vec = got[6:]
-        near, far = reduce_halves(sent, kept)
-        middle, two_own = norm_after(2 * l + 1, stream, near, far, vec)
-        two_other = swap(two_own, "ka", 1)
-        hidden, active, sent, kept = feed_forward(info, two_own, two_other, fc[l], proj[l])
-        saved.append((stream, x_all, projected, attended, lse, middle, two_own, two_other, hidden, active))
-        if l == 0:
-            near, far = reduce_halves(sent, kept)
-            stream, own = norm_after(2, middle, near, far, vec)
-            x = [own, swap(own, "ka", 1)]
-    near = (kept + swap(sent, "ka", 1).astype(F32)).astype(BF)
+    tokens_all, tall, w_fc_in, cotangent_in = tie(tokens_all, tall, w_fc, cotangent)
+    local_fc = lax.dynamic_slice_in_dim(w_fc_in, me * ff_part, ff_part, 2)
+    out0 = Spread(tall[:slot], pb)
+    tall_a = gather_rows(tall[slot : 2 * slot + proj_rows])
+    fc0 = Spread(local_fc[:, 0], pb)
+    tall_b = gather_rows(jnp.concatenate([local_fc[:, 1], tall[2 * slot + proj_rows :]], axis=0))
+    cotangent_all = lax.all_gather(cotangent_in, "ka", axis=0, tiled=True)
+    fc = [None, whole_rows(tall_b, pb, 0, d_rows)]
+    proj = [whole_rows(tall_a, pb, slot, proj_rows, span), whole_rows(tall_b, pb, d_rows, proj_rows, span)]
+    out0.turn(cotangent_all)
+    out = [out0.rows(out_rows, span), whole_rows(tall_a, pb, 0, out_rows, span)]
+
+    def partial_sums(sent, kept):
+        near = (kept + swap(sent, "ka", 1).astype(F32)).astype(BF)
+        return near, swap(near, "ka", 2)
 
     def block(half, which):
         return lax.dynamic_slice_in_dim(half, which * rows, rows, 0)
 
-    far = swap(block(near, 1 - high), "ka", 2)
-    output = (block(middle, high) + (block(near, high).astype(F32) + far.astype(F32))).astype(BF)
+    keys = ("stream", "x", "projected", "attended", "lse", "middle", "own", "other", "hidden", "active")
+    got = attention_forward(True, True, info, kept_all, [tokens_all], qkv[0], out[0], heads)
+    x_all, projected, attended, lse, sent, kept, stream, vec = got
+    near, far = partial_sums(sent, kept)
+    fc0.turn(near)
+    fc[0] = fc0.rows()
+    second = jnp.concatenate([local_qkv(1), jnp.zeros((d_rows, wide - 3 * part), BF)], axis=1)
+    second, unused = tie(second, near)
+    qkv1 = Spread(second, pb)
+    middle, own = norm_after(1, stream, near, far, vec)
+    other = swap(own, "ka", 1)
+    hidden, active, sent, kept = feed_forward(info, own, other, fc[0], proj[0])
+    kept0 = dict(zip(keys, (stream, x_all, projected, attended, lse, middle, own, other, hidden, active)))
+    near, far = partial_sums(sent, kept)
+    qkv1.turn(near)
+    qkv[1] = qkv1.rows()
+    stream, own = norm_after(2, middle, near, far, vec)
+    other = swap(own, "ka", 1)
+    got = attention_forward(False, False, info, kept_all, [own, other], qkv[1], out[1], heads)
+    x_all, projected, attended, lse, sent, kept = got
+    near, far = partial_sums(sent, kept)
+    middle, own = norm_after(3, stream, near, far, vec)
+    other = swap(own, "ka", 1)
+    hidden, active, last_sent, last_kept = feed_forward(info, own, other, fc[1], proj[1])
+    kept1 = dict(zip(keys, (stream, x_all, projected, attended, lse, middle, own, other, hidden, active)))
 
     cot = cotangent_all.reshape(2, 2, rows, width)
     branch = [lax.dynamic_index_in_dim(cot, i, 1, False).reshape(2 * rows, width) for i in (low, 1 - low)]
-    grad = branch[0]
     sums = [None] * 4
-    flows = []
-    held = []
-    for l in (1, 0):
-        stream, x_all, projected, attended, lse, middle, two_own, two_other, hidden, active = saved[l]
-        grad_hidden, sent, kept = feed_backward(info, branch[0], branch[1], hidden, fc[l], proj[l])
-        two = jnp.concatenate([two_own, two_other], axis=0)
-        branch_all = jnp.concatenate(branch, axis=0)
-        held = [(two, grad_hidden), (active, branch_all)] + held
-        if l:
-            flows.append(sum_rows(info, held, pb))
-            held = []
-        near, far = reduce_halves(sent, kept)
-        grad, grad_low, sums[2 * l + 1] = norm_back(2 * l + 1, grad, near, far, middle, vec)
-        other = swap(grad_low, "ka", 1)
-        middle_all, grad_projected, sent, kept = attention_backward(l == 0, info, kept_all, grad_low, other, projected, lse, qkv[l], out[l], heads)
-        held = held + [(attended, middle_all)]
-        if l == 0:
-            flows.append(sum_rows(info, held, pb))
-        flows.append(sum_rows(info, [(x_all, grad_projected)], pb))
-        near, far = reduce_halves(sent, kept)
-        grad, grad_low, sums[2 * l] = norm_back(2 * l, grad, near, far, stream, vec)
-        branch = [grad_low, swap(grad_low, "ka", 1)]
-    grad_tokens = block(grad, high)
-
-    def cut(flow, *sizes):
-        start, found = 0, []
-        for size in sizes:
-            found.append(flow[start : start + size])
-            start += slot_of(size)
-        return found
-
-    fc1, proj1 = cut(flows[0], d_rows, proj_rows)
-    (qkv1,) = cut(flows[1], d_rows)
-    fc0, proj0, out1, out0 = cut(flows[2], d_rows, proj_rows, out_rows, out_rows)
-    (qkv0,) = cut(flows[3], d_rows)
+    half, group = 2 * rows, 4 * rows
+
+    def fc_pair(kept, grad_hidden):
+        return [(kept["own"], 0, grad_hidden, 0, half), (kept["other"], 0, grad_hidden, half, half)], 0
+
+    def proj_pair(kept, branch):
+        return [(kept["active"], 0, branch[0], 0, half), (kept["active"], half, branch[1], 0, half)], span
+
+    def attend_back(l, kept, own):
+        return attention_backward(
+            l == 0, l == 0, info, kept_all, own, swap(own, "ka", 1), kept["projected"], kept["lse"], qkv[l], out[l], tokens_all, heads
+        )
+
+    grad_hidden, sent, kept = feed_backward(info, branch[0], branch[1], kept1["hidden"], fc[1], proj[1])
+    near, far = partial_sums(sent, kept)
+    near_in, grad_hidden, last_sent, last_kept = tie(near, grad_hidden, last_sent, last_kept)
+    last = (last_kept + swap(last_sent, "ka", 1).astype(F32)).astype(BF)
+    last_far = swap(block(last, 1 - high), "ka", 2)
+    flow_a = Flow(info, [fc_pair(kept1, grad_hidden), proj_pair(kept1, branch)], pb)
+    far, unused = tie(far, flow_a.made)
+    grad, own, sums[3] = norm_back(3, branch[0], near, far, kept1["middle"], vec)
+    middle_all1, grad_projected, sent, kept = attend_back(1, kept1, own)
+    near, far = partial_sums(sent, kept)
+    near_in, grad_projected, last_far = tie(near, grad_projected, last_far)
+    output = (block(kept1["middle"], high) + (block(last, high).astype(F32) + last_far.astype(F32))).astype(BF)
+    flow_b = Flow(info, [([(kept1["x"], 0, grad_projected, 0, group)], 0)], pb)
+    flow_a.turn(near)
+    far, unused = tie(far, flow_b.made)
+    grad, own, sums[2] = norm_back(2, grad, near, far, kept1["stream"], vec)
+    branch = [own, swap(own, "ka", 1)]
+    grad_hidden, sent, kept = feed_backward(info, branch[0], branch[1], kept0["hidden"], fc[0], proj[0])
+    near, far = partial_sums(sent, kept)
+    near_in, grad_hidden, middle_all1 = tie(near, grad_hidden, middle_all1)
+    flow_c = Flow(info, [fc_pair(kept0, grad_hidden)], pb)
+    flow_d = Flow(info, [proj_pair(kept0, branch), ([(kept1["attended"], 0, middle_all1, 0, group)], span)], pb)
+    flow_b.turn(near)
+    far, *unused = tie(far, flow_c.made, flow_d.made)
+    grad, own, sums[1] = norm_back(1, grad, near, far, kept0["middle"], vec)
+    fc_proj1 = flow_a.end(own)
+    middle_all, grad_projected, sent, kept, sums[0] = attend_back(0, kept0, own)
+    near = (kept + swap(sent, "ka", 1).astype(F32)).astype(BF)
+    far = swap(block(near, 1 - high), "ka", 2)
+    near_in, grad_projected, middle_all = tie(near, grad_projected, middle_all)
+    flow_f = Flow(info, [([(kept0["attended"], 0, middle_all, 0, group)], span)], pb)
+    halved = [sums[0]] + [0.5 * s for s in sums[1:]]
+    stacked = jnp.concatenate([s[i : i + 1] for i in range(2) for s in halved] + [jnp.zeros((8, width), F32)], axis=0).astype(BF)
+    spots = (3 * part + jnp.arange(16)[:, None] == jnp.arange(wide)[None, :]) & (jnp.arange(16)[:, None] < 8)
+    flow_e = Flow(info, [([(kept0["x"], 0, grad_projected, 0, group), (stacked, 0, spots.astype(BF), 0, 16)], 0)], pb)
+    flow_c.turn(near)
+    (grad_tokens,) = norm_back(0, block(grad, high), block(near, high), far, block(kept0["stream"], high), vec, True)
+
     back = [(b, a) for a, b in moves]
-    proj1 = lax.ppermute(proj1, ("pb", "ka"), back)
-    tall = lax.ppermute(jnp.concatenate([proj0, out0, out1], axis=0), ("pb", "ka"), back)
-    late = lax.all_gather(jnp.concatenate([fc1, proj1], axis=0), "ka", axis=0)
-    early = lax.all_gather(jnp.concatenate([fc0, tall], axis=0), "ka", axis=0)
-    qkvs = [lax.all_gather(v, "ka", axis=0)[:, :, : 3 * part].reshape(ka, d_rows, 3, part).transpose(1, 2, 0, 3).reshape(d_rows, 3 * width) for v in (qkv0, qkv1)]
-    fcs = [v[:, :d_rows].transpose(1, 0, 2).reshape(d_rows, ff) for v in (early, late)]
-    projs = [v[:, d_rows : d_rows + proj_rows].reshape(-1, width) for v in (early, late)]
-    outs = [early[:, d_rows + proj_rows + i * out_rows : d_rows + proj_rows + (i + 1) * out_rows].reshape(-1, width) for i in range(2)]
-    summed = [jnp.stack(v, axis=1).astype(F32) for v in (qkvs, outs, fcs, projs)]
-    stacked = jnp.concatenate(sums, axis=0) * 0.5
-    stacked = lax.psum(stacked, ("pb", "ka"))
-    stacked = lax.dynamic_slice_in_dim(stacked, lax.axis_index("pb") * d_rows, d_rows, 1)
-    stacked = stacked.reshape(4, 2, d_rows)
-    return (output, grad_tokens, *summed, stacked[:, 0].T, stacked[:, 1].T)
+    proj1 = lax.ppermute(fc_proj1[slot_of(d_rows) :], ("pb", "ka"), back)
+    wide1 = gather_ka(jnp.concatenate([fc_proj1[: slot_of(d_rows)], proj1], axis=0))
+    qkv1 = gather_ka(flow_b.end(near))
+    flow_d.turn(flow_e.made)
+    fc0 = gather_ka(flow_c.end(flow_e.made))
+    flow_f.turn(flow_d.kept)
+    flow_e.turn(flow_d.kept)
+    tall0 = gather_ka(lax.ppermute(flow_d.end(flow_e.kept), ("pb", "ka"), back))
+    tall1 = gather_ka(lax.ppermute(flow_f.end(flow_e.kept), ("pb", "ka"), back))
+    qkv0 = gather_ka(flow_e.end(flow_e.kept))
+
+    def columns(pieces):
+        return jnp.concatenate([p[:d_rows] for p in pieces], axis=1)
+
+    def heads_of(pieces):
+        return jnp.concatenate([p[:d_rows, i * part : (i + 1) * part] for i in range(3) for p in pieces], axis=1)
+
+    def rows_of(pieces, start, size):
+        return jnp.concatenate([p[start : start + size] for p in pieces], axis=0)
+
+    shift = slot_of(d_rows)
+    summed = (
+        (heads_of(qkv0), heads_of(qkv1)),
+        (rows_of(tall1, 0, out_rows), rows_of(tall0, slot_of(proj_rows), out_rows)),
+        (columns(fc0), columns(wide1)),
+        (rows_of(tall0, 0, proj_rows), rows_of(wide1, shift, proj_rows)),
+    )
+    summed = [jnp.stack(pair, axis=1).astype(F32) for pair in summed]
+    stacked = sum(p[:d_rows, 3 * part : 3 * part + 8].astype(F32) for p in qkv0)
+    return (output, grad_tokens, *summed, stacked[:, :4], stacked[:, 4:])
 
 
 def solution(mesh):

time: 536 us -> 443 us (0.83)
  waiting for transfers between devices: 211 us -> 149 us
  blocking collectives: 85 us -> 37 us
  starting transfers between devices: 86.3 us -> 95.9 us
  local copies, waits for them, and re-layouts: 55.6 us -> 63.4 us
    psum x1 -> x0, blocking collectives: 39.8 us -> none  [on_device(): stacked = lax.psum(stacked, ('pb', 'ka'))]
    ppermute x50 -> x77, waiting for transfers between devices: 188 us -> 149 us  [swap(): return lax.ppermute(x, axis, [(i, i ^ bit) for i in range(size)])]
    all_gather x2, waiting for transfers between devices: 23.1 us -> 0.01 us  [gather_rows(): return lax.all_gather(x, 'pb', axis=0, tiled=True)]
    unnamed x187 -> x248, local copies, waits for them, and re-layouts: 28.9 us -> 40.9 us
    ppermute x50 -> x77, starting transfers between devices: 80.7 us -> 92.4 us  [swap(): return lax.ppermute(x, axis, [(i, i ^ bit) for i in range(size)])]
    all_gather x3 -> x1, blocking collectives: 26.3 us -> 15.1 us  [on_device(): cotangent_all = lax.all_gather(cotangent_in, 'ka', axis=0, tiled=True)]
    concatenate x13 -> x6, other arithmetic: 6.54 us -> 0.96 us  [the longest x1 0.75 us: on_device(): jnp.concatenate([local_fc[:, 1], tall[2 * slot + proj_rows:]], axis=0)]
    all_gather x1, blocking collectives: 11.2 us -> 16.7 us  [on_device(): tokens_all = lax.all_gather(tokens, 'ka', axis=0, tiled=True)]
  transfers between devices with their start and end apart: 57 -> 83, of which waited for: 26 -> 33; matrix products, arithmetic and copies ran while one was open for 9% -> 8% of each run, Pallas kernels for 7% -> 12%
where the time goes in v3:
time: 443 us; the launch traced here: 435 us
  waiting for transfers between devices  149 us (34%)
  starting transfers between devices  95.9 us (22%)
  local copies, waits for them, and re-layouts  63.4 us (14%)
  Pallas kernels  57.7 us (13%)
  blocking collectives  37 us (8%)
  between operations  16.5 us (4%)
  other arithmetic  15.6 us (4%)
    ppermute x77, waiting for transfers between devices, swap(): return lax.ppermute(x, axis, [(i, i ^ bit) for i in range(size)])  149 us
    ppermute x77, starting transfers between devices, swap(): return lax.ppermute(x, axis, [(i, i ^ bit) for i in range(size)])  92.4 us
    pallas_call x21, Pallas kernels, call(): pl.pallas_call(kernel, out_shape=[jax.ShapeDtypeStruct(s, t) for s, t in...  57.7 us
    unnamed x248, local copies, waits for them, and re-layouts  40.9 us
    all_gather x1, blocking collectives, on_device(): tokens_all = lax.all_gather(tokens, 'ka', axis=0, tiled=True)  16.7 us
    all_gather x1, blocking collectives, on_device(): cotangent_all = lax.all_gather(cotangent_in, 'ka', axis=0, tiled=True)  15.1 us
  transfers between devices with their start and end apart: 83, of which 33 were waited for; matrix products, arithmetic and copies ran while one was open for 8% of the time, Pallas kernels for 12%

profile of v3, /device:TPU:0, one launch (start us, length us, event | category | flops | bytes accessed | tf_op | source)
XLA Modules:
  0.0 435.1 jit_solution(9290046222801466778)
XLA Ops:
  8.8 5.3 %slice_reduce_fusion = (bf16[96,2304]{1,0:T(8,128)(2,1)S(1)}, bf16[96,2304]{1,0:T(8,128)(2,1)S(1)}) fusion(bf16[96,2,2304]{2,1,0:T(2,128)(2,1)} %param.14), kind=kLoop, calls=%fused_computation.10 | loop fusion | bytes 1769472 | tf_op jit(solution)/shard_map/slice | solution.py:569
  18.9 16.7 %all_gather.16.refs_2_.refs_19_ = bf16[512,768]{1,0:T(8,128)(2,1)S(1)} all-gather(bf16[128,768]{1,0:T(8,128)(2,1)S(1)} %copy-done.116), channel_id=1, replica_groups=mesh['pb'=8,'ka'=4] {'ka'}, dimensions={0}, use_global_device_ids=true | all-gather | bytes 983040 | tf_op jit(solution)/shard_map/all_gather | solution.py:585
  48.6 15.1 %all_gather.17 = bf16[512,768]{1,0:T(8,128)(2,1)} all-gather(bf16[128,768]{1,0:T(8,128)(2,1)S(1)} %copy-done.117), channel_id=1, replica_groups=mesh['pb'=8,'ka'=4] {'ka'}, dimensions={0}, use_global_device_ids=true | all-gather | bytes 983040 | tf_op jit(solution)/shard_map/all_gather | solution.py:592
  70.3 5.7 %collective-permute-done.5.refs_8_.refs_11_ = bf16[96,640]{1,0:T(8,128)(2,1)S(1)} collective-permute-done((bf16[96,640]{1,0:T(8,128)(2,1)S(1)}, bf16[96,640]{1,0:T(8,128)(2,1)S(1)}, u32[]{:S(2)}, u32[]{:S(2)}) %collective-permute-start.5) | collective-permute-done | bytes 122912 | tf_op jit(solution)/shard_map/ppermute | solution.py:460
  76.8 5.2 %all-gather = s32[4,1,128]{2,1,0:T(1,128)S(1)} all-gather(s32[1,1,128]{2,1,0:T(1,128)S(1)} %bitcast.200), channel_id=1, replica_groups=mesh['pb'=8,'ka'=4] {'ka'}, dimensions={0}, use_global_device_ids=true | all-gather | bytes 2560 | tf_op jit(solution)/shard_map/all_gather | solution.py:584
  91.2 7.3 %attend.2 = (bf16[512,768]{1,0:T(8,128)(2,1)S(1)}, bf16[512,640]{1,0:T(8,128)(2,1)S(1)}, bf16[512,192]{1,0:T(8,128)(2,1)S(1)}, f32[512,128]{1,0:T(8,128)S(1)}, b...) custom-call(s32[5]{0:T(128)S(1)} %pad_add_fusion.refs_0_, ...), custom_call_target="tpu_custom_call" | custom-call | flops 603979776 | bytes 2164756 | tf_op jit(solution)/shard_map/attend/pallas_call | solution.py:26
  113.2 10.3 %collective-permute-done.16.refs_5_.refs_6_ = bf16[96,768]{1,0:T(8,128)(2,1)S(1)} collective-permute-done((bf16[96,768]{1,0:T(8,128)(2,1)S(1)}, bf16[96,768]{1,0:T(8,128)(2,1)S(1)}, u32[]{:S(2)}, u32[]{:S(2)}) %collective-permute-start.16) | collective-permute-done | bytes 147488 | tf_op jit(solution)/shard_map/ppermute | solution.py:460
  128.5 17.7 %collective-permute-done.18.refs_7_.refs_8_ = bf16[384,768]{1,0:T(8,128)(2,1)S(1)} collective-permute-done((bf16[384,768]{1,0:T(8,128)(2,1)S(1)}, bf16[384,768]{1,0:T(8,128)(2,1)S(1)}, u32[]{:S(2)}, u32[]{:S(2)}) %collective-permute-start.18) | collective-permute-done | bytes 589856 | tf_op jit(solution)/shard_map/ppermute | solution.py:460
  160.4 4.6 %collective-permute-done.24.refs_7_.refs_9_ = bf16[96,640]{1,0:T(8,128)(2,1)S(1)} collective-permute-done((bf16[96,640]{1,0:T(8,128)(2,1)S(1)}, bf16[96,640]{1,0:T(8,128)(2,1)S(1)}, u32[]{:S(2)}, u32[]{:S(2)}) %collective-permute-start.24) | collective-permute-done | bytes 122912 | tf_op jit(solution)/shard_map/ppermute | solution.py:460
  164.9 5.2 %collective-permute-done.23.refs_6_.refs_8_ = bf16[96,640]{1,0:T(8,128)(2,1)S(1)} collective-permute-done((bf16[96,640]{1,0:T(8,128)(2,1)S(1)}, bf16[96,640]{1,0:T(8,128)(2,1)S(1)}, u32[]{:S(2)}, u32[]{:S(2)}) %collective-permute-start.23) | collective-permute-done | bytes 122912 | tf_op jit(solution)/shard_map/ppermute | solution.py:460
  174.2 9.3 %collective-permute-done.25.refs_8_.refs_10_ = bf16[384,640]{1,0:T(8,128)(2,1)S(1)} collective-permute-done((bf16[384,640]{1,0:T(8,128)(2,1)S(1)}, bf16[384,640]{1,0:T(8,128)(2,1)S(1)}, u32[]{:S(2)}, u32[]{:S(2)}) %collective-permute-start.25) | collective-permute-done | bytes 491552 | tf_op jit(solution)/shard_map/ppermute | solution.py:460
  183.5 6.3 %attend.3 = (bf16[512,768]{1,0:T(8,128)(2,1)S(1)}, bf16[512,640]{1,0:T(8,128)(2,1)S(1)}, bf16[512,192]{1,0:T(8,128)(2,1)S(1)}, f32[512,128]{1,0:T(8,128)S(1)}, b...) custom-call(s32[5]{0:T(128)S(1)} %pad_add_fusion.refs_0_, s32[1,512]{1,0:T(1,128)S(1)} %bitcast.172, ...), custom_call_target="tpu_custom_call" | custom-call | flops 603979776 | bytes 3344404 | tf_op jit(solution)/shard_map/attend/pallas_call | solution.py:26
  192.8 11.1 %collective-permute-done.27.far = bf16[256,768]{1,0:T(8,128)(2,1)S(1)} collective-permute-done((bf16[256,768]{1,0:T(8,128)(2,1)S(1)}, bf16[256,768]{1,0:T(8,128)(2,1)S(1)}, u32[]{:S(2)}, u32[]{:S(2)}) %collective-permute-start.27) | collective-permute-done | bytes 393248 | tf_op jit(solution)/shard_map/ppermute | solution.py:460
  222.2 6.7 %collective-permute-done.31.far = bf16[256,768]{1,0:T(8,128)(2,1)S(1)} collective-permute-done((bf16[256,768]{1,0:T(8,128)(2,1)S(1)}, bf16[256,768]{1,0:T(8,128)(2,1)S(1)}, u32[]{:S(2)}, u32[]{:S(2)}) %collective-permute-start.31) | collective-permute-done | bytes 393248 | tf_op jit(solution)/shard_map/ppermute | solution.py:460
  241.2 7.5 %attend_back.2 = (bf16[512,768]{1,0:T(8,128)(2,1)S(1)}, bf16[512,640]{1,0:T(8,128)(2,1)S(1)}, bf16[256,768]{1,0:T(8,128)(2,1)S(1)}, f32[256,768]{1,0:T(8,128)S(1)}) custom-call(s32[5]{0:T(128)S(1)} %pad_add_fusion.refs_0_, s32[1,512]{1,0:T(1,128)S(1)} %bitcast.173, bf16[256,768]{1,0:T(8,128)(2,1)} %get-tuple-element.184.refs_2_, ...), custom_call_target="tpu_custom_call" | custom-call | flops 603979776 | bytes 4261908 | tf_op jit(solution)/shard_map/attend_back/pallas_call | solution.py:26
  251.2 5.5 %collective-permute-done.34 = bf16[128,768]{1,0:T(8,128)(2,1)S(1)} collective-permute-done((bf16[128,768]{1,0:T(8,128)(2,1)S(1)}, bf16[128,768]{1,0:T(8,128)(2,1)S(1)}, u32[]{:S(2)}, u32[]{:S(2)}) %collective-permute-start.34) | collective-permute-done | bytes 196640 | tf_op jit(solution)/shard_map/ppermute | solution.py:460
  258.8 4.4 %collective-permute-done.74 = bf16[4,192,768]{2,1,0:T(8,128)(2,1)S(1)} collective-permute-done((bf16[4,192,768]{2,1,0:T(8,128)(2,1)}, bf16[4,192,768]{2,1,0:T(8,128)(2,1)S(1)}, u32[]{:S(2)}, u32[]{:S(2)}) %collective-permute-start.74) | collective-permute-done | bytes 1179680 | tf_op jit(solution)/shard_map/ppermute | solution.py:460
  289.4 9.1 %collective-permute-done.76 = bf16[192,768]{1,0:T(8,128)(2,1)S(1)} collective-permute-done((bf16[192,768]{1,0:T(8,128)(2,1)S(1)}, bf16[192,768]{1,0:T(8,128)(2,1)S(1)}, u32[]{:S(2)}, u32[]{:S(2)}) %collective-permute-start.76) | collective-permute-done | bytes 294944 | tf_op jit(solution)/shard_map/ppermute | solution.py:460
  301.4 10.7 %collective-permute-start.79 = (bf16[192,768]{1,0:T(8,128)(2,1)}, bf16[192,768]{1,0:T(8,128)(2,1)}, u32[]{:S(2)}, u32[]{:S(2)}) collective-permute-start(bf16[192,768]{1,0:T(8,128)(2,1)} %get-tuple-element.355), channel_id=1, source_target_pairs={{0,2},{1,3},{2,0},{3,1},{4,6},{5,7},{6,4},{7,5},{8,10},{9,11},{10,... | collective-permute-start | bytes 884744 | tf_op jit(solution)/shard_map/ppermute | solution.py:460
  312.2 8.0 %attend_back.3 = (bf16[512,768]{1,0:T(8,128)(2,1)S(1)}, bf16[512,640]{1,0:T(8,128)(2,1)S(1)}, bf16[256,768]{1,0:T(8,128)(2,1)}, f32[256,768]{1,0:T(8,128)S(1)}, f32[2,768]{1,0:T(2,128)S(1)}) custom-call(s32[5]{0:T(128)S(1)} %pad_add_fusion.refs_0_, s32[1,512]{1,0:T(1,128)S(1)} %bitcast.174, bf16[256,768]{1,0:T(8,128)(2,1)S(1)} %get-tuple-element.211.refs_2_, ...), custom_call_target="tpu_custom_call" | custom-call | flops 603979776 | bytes 3868692 | tf_op jit(solution)/shard_map/attend_back/pallas_call | solution.py:26
  327.6 10.8 %collective-permute-done.68 = bf16[4,96,768]{2,1,0:T(8,128)(2,1)S(1)} collective-permute-done((bf16[4,96,768]{2,1,0:T(8,128)(2,1)}, bf16[4,96,768]{2,1,0:T(8,128)(2,1)S(1)}, u32[]{:S(2)}, u32[]{:S(2)}) %collective-permute-start.68) | collective-permute-done | bytes 589856 | tf_op jit(solution)/shard_map/ppermute | solution.py:460
  341.7 12.2 %collective-permute-done.42 = bf16[4,128,768]{2,1,0:T(8,128)(2,1)S(1)} collective-permute-done((bf16[4,128,768]{2,1,0:T(8,128)(2,1)S(1)}, bf16[4,128,768]{2,1,0:T(8,128)(2,1)S(1)}, u32[]{:S(2)}, u32[]{:S(2)}) %collective-permute-start.42) | collective-permute-done | bytes 786464 | tf_op jit(solution)/shard_map/ppermute | solution.py:460
  393.9 8.3 %collective-permute-start.60 = (bf16[32,768]{1,0:T(8,128)(2,1)S(1)}, bf16[32,768]{1,0:T(8,128)(2,1)S(1)}, u32[]{:S(2)}, u32[]{:S(2)}) collective-permute-start(bf16[32,768]{1,0:T(8,128)(2,1)S(1)} %collective-permute-done.59), channel_id=1, source_target_pairs={{0,2},{1,3},{2,0},{3,1},{4,6},{5,7},{6,4},{7,5},{8,10},{9,11},{10,... | collective-permute-start | bytes 147464 | tf_op jit(solution)/shard_map/ppermute | solution.py:460
  408.2 5.4 %collective-permute-start.66 = (bf16[128,768]{1,0:T(8,128)(2,1)S(1)}, bf16[128,768]{1,0:T(8,128)(2,1)S(1)}, u32[]{:S(2)}, u32[]{:S(2)}) collective-permute-start(bf16[128,768]{1,0:T(8,128)(2,1)S(1)} %collective-permute-done.65), channel_id=1, source_target_pairs={{0,2},{1,3},{2,0},{3,1},{4,6},{5,7},{6,4},{7,5},{8,10},{9,11},{10,... | collective-permute-start | bytes 589832 | tf_op jit(solution)/shard_map/ppermute | solution.py:460
  (552 shorter events, 210.3 us)
Async XLA Ops:
  7.2 139.1 %all-gather.4.cloned.1.call-start = ((), (), s32[]{:S(2)}) async-start(), calls=%async_computation | async-start | bytes 1769472 | tf_op jit(solution)/shard_map/all_gather | solution.py:469
  36.4 171.5 %all-gather.6.cloned.1.call-start = ((), (), s32[]{:S(2)}) async-start(), calls=%async_computation.1 | async-start | bytes 2654208 | tf_op jit(solution)/shard_map/all_gather | solution.py:469
  36.4 31.8 %collective-permute-start.7 = (bf16[96,640]{1,0:T(8,128)(2,1)S(1)}, bf16[96,640]{1,0:T(8,128)(2,1)S(1)}, u32[]{:S(2)}, u32[]{:S(2)}) collective-permute-start(bf16[96,640]{1,0:T(8,128)(2,1)S(1)} %maximum_maximum_fusion.refs_3_.refs_6_), channel_id=1, source_target_pairs={{0,28},{4,24},{8,20},{12,16},{16,12},{20,8},{24,4},{28,0},{1,29},{... | collective-permute-start | bytes 368648 | tf_op jit(solution)/shard_map/ppermute | solution.py:460
  40.7 29.0 %collective-permute-start.6 = (bf16[96,640]{1,0:T(8,128)(2,1)S(1)}, bf16[96,640]{1,0:T(8,128)(2,1)S(1)}, u32[]{:S(2)}, u32[]{:S(2)}) collective-permute-start(bf16[96,640]{1,0:T(8,128)(2,1)S(1)} %maximum_maximum_fusion.refs_3_.refs_6_), channel_id=1, source_target_pairs={{0,24},{4,28},{8,16},{12,20},{16,8},{20,12},{24,0},{28,4},{1,25},{... | collective-permute-start | bytes 368648 | tf_op jit(solution)/shard_map/ppermute | solution.py:460
  41.2 22.5 %collective-permute-start.10 = (bf16[32,768]{1,0:T(8,128)(2,1)S(1)}, bf16[32,768]{1,0:T(8,128)(2,1)S(1)}, u32[]{:S(2)}, u32[]{:S(2)}) collective-permute-start(bf16[32,768]{1,0:T(8,128)(2,1)S(1)} %slice.426.refs_11_.refs_14_), channel_id=1, source_target_pairs={{0,24},{4,28},{8,16},{12,20},{16,8},{20,12},{24,0},{28,4},{1,25},{... | collective-permute-start | bytes 147464 | tf_op jit(solution)/shard_map/ppermute | solution.py:460
  44.6 19.9 %collective-permute-start.9 = (bf16[32,768]{1,0:T(8,128)(2,1)S(1)}, bf16[32,768]{1,0:T(8,128)(2,1)S(1)}, u32[]{:S(2)}, u32[]{:S(2)}) collective-permute-start(bf16[32,768]{1,0:T(8,128)(2,1)S(1)} %slice.426.refs_11_.refs_14_), channel_id=1, source_target_pairs={{0,16},{4,20},{8,24},{12,28},{16,0},{20,4},{24,8},{28,12},{1,17},{... | collective-permute-start | bytes 147464 | tf_op jit(solution)/shard_map/ppermute | solution.py:460
  64.5 24.9 %collective-permute-start.11 = (bf16[128,768]{1,0:T(8,128)(2,1)S(1)}, bf16[128,768]{1,0:T(8,128)(2,1)S(1)}, u32[]{:S(2)}, u32[]{:S(2)}) collective-permute-start(bf16[128,768]{1,0:T(8,128)(2,1)S(1)} %pad_maximum_fusion.9), channel_id=1, source_target_pairs={{0,4},{4,0},{8,12},{12,8},{16,20},{20,16},{24,28},{28,24},{1,5},{5... | collective-permute-start | bytes 589832 | tf_op jit(solution)/shard_map/ppermute | solution.py:460
  104.6 18.9 %collective-permute-start.16 = (bf16[96,768]{1,0:T(8,128)(2,1)S(1)}, bf16[96,768]{1,0:T(8,128)(2,1)S(1)}, u32[]{:S(2)}, u32[]{:S(2)}) collective-permute-start(bf16[96,768]{1,0:T(8,128)(2,1)S(1)} %get-tuple-element.155.refs_3_.refs_4_), channel_id=1, source_target_pairs={{0,16},{4,20},{8,24},{12,28},{16,0},{20,4},{24,8},{28,12},{1,17},{... | collective-permute-start | bytes 442376 | tf_op jit(solution)/shard_map/ppermute | solution.py:460
  124.2 22.0 %collective-permute-start.18 = (bf16[384,768]{1,0:T(8,128)(2,1)S(1)}, bf16[384,768]{1,0:T(8,128)(2,1)S(1)}, u32[]{:S(2)}, u32[]{:S(2)}) collective-permute-start(bf16[384,768]{1,0:T(8,128)(2,1)S(1)} %pad_maximum_fusion), channel_id=1, source_target_pairs={{0,4},{4,0},{8,12},{12,8},{16,20},{20,16},{24,28},{28,24},{1,5},{5... | collective-permute-start | bytes 1769480 | tf_op jit(solution)/shard_map/ppermute | solution.py:460
  234.1 29.1 %collective-permute-start.74 = (bf16[4,192,768]{2,1,0:T(8,128)(2,1)}, bf16[4,192,768]{2,1,0:T(8,128)(2,1)S(1)}, u32[]{:S(2)}, u32[]{:S(2)}) collective-permute-start(bf16[4,192,768]{2,1,0:T(8,128)(2,1)} %copy-done.87), channel_id=1, source_target_pairs={{0,4},{4,0},{8,12},{12,8},{16,20},{20,16},{24,28},{28,24},{1,5},{5... | collective-permute-start | bytes 3538952 | tf_op jit(solution)/shard_map/ppermute | solution.py:460
  265.6 21.8 %collective-permute-start.77 = (bf16[192,768]{1,0:T(8,128)(2,1)S(1)}, bf16[192,768]{1,0:T(8,128)(2,1)S(1)}, u32[]{:S(2)}, u32[]{:S(2)}) collective-permute-start(bf16[192,768]{1,0:T(8,128)(2,1)S(1)} %get-tuple-element.298), channel_id=1, source_target_pairs={{0,24},{4,28},{8,16},{12,20},{16,8},{20,12},{24,0},{28,4},{1,25},{... | collective-permute-start | bytes 884744 | tf_op jit(solution)/shard_map/ppermute | solution.py:460
  267.1 31.4 %collective-permute-start.76 = (bf16[192,768]{1,0:T(8,128)(2,1)S(1)}, bf16[192,768]{1,0:T(8,128)(2,1)S(1)}, u32[]{:S(2)}, u32[]{:S(2)}) collective-permute-start(bf16[192,768]{1,0:T(8,128)(2,1)S(1)} %get-tuple-element.299), channel_id=1, source_target_pairs={{0,16},{4,20},{8,24},{12,28},{16,0},{20,4},{24,8},{28,12},{1,17},{... | collective-permute-start | bytes 884744 | tf_op jit(solution)/shard_map/ppermute | solution.py:460
  267.1 31.4 %collective-permute-start.75 = (bf16[192,768]{1,0:T(8,128)(2,1)S(1)}, bf16[192,768]{1,0:T(8,128)(2,1)S(1)}, u32[]{:S(2)}, u32[]{:S(2)}) collective-permute-start(bf16[192,768]{1,0:T(8,128)(2,1)S(1)} %get-tuple-element.300), channel_id=1, source_target_pairs={{0,8},{4,12},{8,0},{12,4},{16,24},{20,28},{24,16},{28,20},{1,9},{5... | collective-permute-start | bytes 884744 | tf_op jit(solution)/shard_map/ppermute | solution.py:460
  276.7 49.5 %collective-permute-start.52 = (bf16[96,640]{1,0:T(8,128)(2,1)}, bf16[96,640]{1,0:T(8,128)(2,1)}, u32[]{:S(2)}, u32[]{:S(2)}) collective-permute-start(bf16[96,640]{1,0:T(8,128)(2,1)} %get-tuple-element.336), channel_id=1, source_target_pairs={{0,24},{4,28},{8,16},{12,20},{16,8},{20,12},{24,0},{28,4},{1,25},{... | collective-permute-start | bytes 368648 | tf_op jit(solution)/shard_map/ppermute | solution.py:460
  286.6 39.7 %collective-permute-start.51 = (bf16[96,640]{1,0:T(8,128)(2,1)}, bf16[96,640]{1,0:T(8,128)(2,1)}, u32[]{:S(2)}, u32[]{:S(2)}) collective-permute-start(bf16[96,640]{1,0:T(8,128)(2,1)} %get-tuple-element.337), channel_id=1, source_target_pairs={{0,16},{4,20},{8,24},{12,28},{16,0},{20,4},{24,8},{28,12},{1,17},{... | collective-permute-start | bytes 368648 | tf_op jit(solution)/shard_map/ppermute | solution.py:460
  287.3 39.0 %collective-permute-start.50 = (bf16[96,640]{1,0:T(8,128)(2,1)}, bf16[96,640]{1,0:T(8,128)(2,1)}, u32[]{:S(2)}, u32[]{:S(2)}) collective-permute-start(bf16[96,640]{1,0:T(8,128)(2,1)} %get-tuple-element.338), channel_id=1, source_target_pairs={{0,8},{4,12},{8,0},{12,4},{16,24},{20,28},{24,16},{28,20},{1,9},{5... | collective-permute-start | bytes 368648 | tf_op jit(solution)/shard_map/ppermute | solution.py:460
  301.4 20.4 %collective-permute-start.79 = (bf16[192,768]{1,0:T(8,128)(2,1)}, bf16[192,768]{1,0:T(8,128)(2,1)}, u32[]{:S(2)}, u32[]{:S(2)}) collective-permute-start(bf16[192,768]{1,0:T(8,128)(2,1)} %get-tuple-element.355), channel_id=1, source_target_pairs={{0,2},{1,3},{2,0},{3,1},{4,6},{5,7},{6,4},{7,5},{8,10},{9,11},{10,... | collective-permute-start | bytes 884744 | tf_op jit(solution)/shard_map/ppermute | solution.py:460
  323.4 30.6 %collective-permute-start.42 = (bf16[4,128,768]{2,1,0:T(8,128)(2,1)S(1)}, bf16[4,128,768]{2,1,0:T(8,128)(2,1)S(1)}, u32[]{:S(2)}, u32[]{:S(2)}) collective-permute-start(bf16[4,128,768]{2,1,0:T(8,128)(2,1)S(1)} %copy-done.91), channel_id=1, source_target_pairs={{0,4},{4,0},{8,12},{12,8},{16,20},{20,16},{24,28},{28,24},{1,5},{5... | collective-permute-start | bytes 2359304 | tf_op jit(solution)/shard_map/ppermute | solution.py:460
  326.2 41.3 %collective-permute-start.80 = (bf16[2,192,768]{2,1,0:T(8,128)(2,1)S(1)}, bf16[2,192,768]{2,1,0:T(8,128)(2,1)S(1)}, u32[]{:S(2)}, u32[]{:S(2)}) collective-permute-start(bf16[2,192,768]{2,1,0:T(8,128)(2,1)S(1)} %pad_maximum_fusion.1), channel_id=1, source_target_pairs={{0,1},{1,0},{2,3},{3,2},{4,5},{5,4},{6,7},{7,6},{8,9},{9,8},{10,11... | collective-permute-start | bytes 1769480 | tf_op jit(solution)/shard_map/ppermute | solution.py:460
  327.5 28.7 %collective-permute-start.53 = (bf16[96,640]{1,0:T(8,128)(2,1)S(1)}, bf16[96,640]{1,0:T(8,128)(2,1)S(1)}, u32[]{:S(2)}, u32[]{:S(2)}) collective-permute-start(bf16[96,640]{1,0:T(8,128)(2,1)S(1)} %add_convert_fusion.18), channel_id=1, source_target_pairs={{0,2},{1,3},{2,0},{3,1},{4,6},{5,7},{6,4},{7,5},{8,10},{9,11},{10,... | collective-permute-start | bytes 368648 | tf_op jit(solution)/shard_map/ppermute | solution.py:460
  356.6 23.0 %collective-permute-start.43 = (bf16[4,96,640]{2,1,0:T(8,128)(2,1)}, bf16[4,96,640]{2,1,0:T(8,128)(2,1)S(1)}, u32[]{:S(2)}, u32[]{:S(2)}) collective-permute-start(bf16[4,96,640]{2,1,0:T(8,128)(2,1)} %get-tuple-element.228), channel_id=1, source_target_pairs={{0,4},{4,0},{8,12},{12,8},{16,20},{20,16},{24,28},{28,24},{1,5},{5... | collective-permute-start | bytes 1474568 | tf_op jit(solution)/shard_map/ppermute | solution.py:460
  359.1 26.9 %collective-permute-start.64 = (bf16[128,768]{1,0:T(8,128)(2,1)}, bf16[128,768]{1,0:T(8,128)(2,1)}, u32[]{:S(2)}, u32[]{:S(2)}) collective-permute-start(bf16[128,768]{1,0:T(8,128)(2,1)} %get-tuple-element.308), channel_id=1, source_target_pairs={{0,24},{4,28},{8,16},{12,20},{16,8},{20,12},{24,0},{28,4},{1,25},{... | collective-permute-start | bytes 589832 | tf_op jit(solution)/shard_map/ppermute | solution.py:460
  364.0 26.2 %collective-permute-start.63 = (bf16[128,768]{1,0:T(8,128)(2,1)}, bf16[128,768]{1,0:T(8,128)(2,1)}, u32[]{:S(2)}, u32[]{:S(2)}) collective-permute-start(bf16[128,768]{1,0:T(8,128)(2,1)} %get-tuple-element.309), channel_id=1, source_target_pairs={{0,16},{4,20},{8,24},{12,28},{16,0},{20,4},{24,8},{28,12},{1,17},{... | collective-permute-start | bytes 589832 | tf_op jit(solution)/shard_map/ppermute | solution.py:460
  386.0 19.9 %collective-permute-start.46 = (bf16[96,640]{1,0:T(8,128)(2,1)S(1)}, bf16[96,640]{1,0:T(8,128)(2,1)S(1)}, u32[]{:S(2)}, u32[]{:S(2)}) collective-permute-start(bf16[96,640]{1,0:T(8,128)(2,1)S(1)} %get-tuple-element.330), channel_id=1, source_target_pairs={{0,24},{4,28},{8,16},{12,20},{16,8},{20,12},{24,0},{28,4},{1,25},{... | collective-permute-start | bytes 368648 | tf_op jit(solution)/shard_map/ppermute | solution.py:460
  (180 other events, 1967.5 us)
Sparse Core Ops, SparseCore 0:
  36.5 59.5 all-gather.3
  104.6 63.8 all-gather.5
